TPU v7x, 32 devices: a whole 2x2x4 slice. The times are simulated.
32 devices in a mesh: space: 16 (over z, y, x), sub: 2 (over core).
Axes of the slice: x: 2, y: 2, z: 4, core: 2. Of those that a mesh axis runs over, the one named last changes fastest.
Arguments:
- fluid_state: float32 [8, 65536], P(None, 'space'), may hold values from 0 to 1
- sphere_state: float32 [7, 65536], P(None, 'space'), may hold values from 0 to 1
- sphere_offset: float32 [3, 65536], P(None, 'space'), may hold values from -1 to 1
- tile_list: int32 [4096, 2], P(('space', 'sub')), may hold values from 0 to 31, as said below
- tile_count: int32 [32], P(('space', 'sub')), may hold values from 32 to 128, as said below
- clump_ids: int32 [65536], P('space'), may hold values from 0 to 127, as said below
- clump_state: float32 [6, 2048], P(None, 'space'), may hold values from -6 to 6
- clump_inverse: float32 [4, 2048], P(None, 'space'), may hold values from 0.02 to 0.2
Outputs:
- clump_velocity: float32 [6, 2048], P(None, 'space')
- sphere_velocity: float32 [3, 65536], P(None, 'space')
Inputs may be any that keep to these rules, and one draw needn't show every extreme that they name: `tile_list`: within a domain the 256 slots of its two devices name distinct pairs; the first entry is below 32, the second below 32. `tile_count`: some device's list is full in every draw. `clump_ids`: among the spheres sent to one owner from all domains, each clump id names exactly 32 spheres.
All inputs are finite; a program needn't handle non-finite values.
Results may differ from a plain program's by a relative error of at most 0.0003.
Values sent between devices are 32-bit elements; how exact they have to be, the bound alone decides.
No kernel may reach another device: no remote copies, remote signals or barrier semaphores. Data moves between devices by JAX's collectives and lax.ppermute only.
A program may use at most 64 MiB of HBM per device.

v0:
```python
import functools
import math

import jax
import jax.numpy as jnp
from jax import lax
from jax.experimental import pallas as pl
from jax.experimental.pallas import tpu as pltpu
from jax.sharding import PartitionSpec as P

TILE = 128
SLOT = 256
UNROLL = 8

support_radius = 0.5
press_coef = 4.0
visc_coef = 1.0
gravity_step = 0.1

f32 = jnp.float32
bf16 = jnp.bfloat16


def split_two(value):
    high = value.astype(bf16)
    return high, (value - high.astype(f32)).astype(bf16)


def cross(left, right):
    return [
        left[1] * right[2] - left[2] * right[1],
        left[2] * right[0] - left[0] * right[2],
        left[0] * right[1] - left[1] * right[0],
    ]


def group_of(owners):
    return math.gcd(owners, 16)


def loads_kernel(
    count_ref, list_hbm, fluid_hbm, sphere_hbm, offset_hbm, ids_hbm, state_hbm, inverse_hbm,
    keep_ref, send_ref,
    list_ref, fluid_ref, sphere_ref, offset_ref, ids_ref, state_ref, inverse_ref, arrived,
    place_ref, wide_ref, terms_ref, weight_ref, acc_ref,
):
    fluid_tiles = fluid_ref.shape[1] // TILE
    clumps = keep_ref.shape[1]
    owners = keep_ref.shape[0] // 3
    core = lax.axis_index("sub")
    me = jnp.where(core == 0, lax.axis_index("space"), -1)

    pairs = (
        (fluid_hbm, fluid_ref),
        (sphere_hbm, sphere_ref),
        (list_hbm, list_ref),
        (offset_hbm, offset_ref),
        (ids_hbm, ids_ref),
        (state_hbm, state_ref),
        (inverse_hbm, inverse_ref),
    )
    copies = [
        pltpu.make_async_copy(source, target, arrived.at[k]) for k, (source, target) in enumerate(pairs)
    ]
    for copy in copies:
        copy.start()

    acc_ref[...] = jnp.zeros_like(acc_ref)
    copies[0].wait()

    @pl.loop(0, fluid_tiles, unroll=8)
    def _(tile):
        cols = pl.ds(pl.multiple_of(tile * TILE, TILE), TILE)
        state = fluid_ref[:, cols]
        row = lax.broadcasted_iota(jnp.int32, state.shape, 0)
        state = jnp.where(row < 3, state * (1.0 / support_radius) - 1.0, state)
        mass = state[7:8]
        first = jnp.where(row < 7, state * mass, state)
        second = jnp.where(row < 3, state * (mass * state[6:7]), 0.0)
        high, low = split_two(jnp.concatenate([first, second], axis=0))
        both = jnp.concatenate([high, low], axis=0)
        terms_ref[tile] = jnp.concatenate([both, both], axis=1)
        turned = state.T
        for k in range(3):
            wide_ref[k, cols, :] = jnp.broadcast_to(turned[:, k : k + 1], (TILE, TILE))

    copies[1].wait()
    place_ref[...] = sphere_ref[0:3, :] * (1.0 / support_radius) - 1.0
    copies[2].wait()

    def pair_weights(slot, part):
        a = list_ref[0, slot]
        b = list_ref[1, slot]
        cols = pl.ds(pl.multiple_of(a * TILE, TILE), TILE)
        rows = pl.ds(pl.multiple_of(b * TILE, TILE), TILE)
        dx = place_ref[0:1, cols] - wide_ref[0, rows, :]
        dy = place_ref[1:2, cols] - wide_ref[1, rows, :]
        dz = place_ref[2:3, cols] - wide_ref[2, rows, :]
        square = jnp.maximum(dx * dx + dy * dy + dz * dz, 1e-30)
        falloff = jnp.maximum(1.0 - square * lax.rsqrt(square), 0.0)
        high, low = split_two(falloff * falloff * falloff)
        weight_ref[part, 0:TILE, :] = high
        weight_ref[part, TILE:, :] = low

    def add_sums(slot, part, live):
        a = list_ref[0, slot]
        b = list_ref[1, slot]
        cols = pl.ds(pl.multiple_of(a * TILE, TILE), TILE)
        sums = jnp.dot(terms_ref[b], weight_ref[part], preferred_element_type=f32)
        acc_ref[:, cols] += live * (sums[0:16] + sums[16:32])

    count = count_ref[0]
    trips = (count + UNROLL - 1) // UNROLL
    last = list_ref.shape[1] - 1

    for part in range(UNROLL):
        pair_weights(min(part, last), part)

    @pl.loop(1, trips)
    def _(trip):
        for part in range(UNROLL):
            add_sums((trip - 1) * UNROLL + part, part, 1.0)
        for part in range(UNROLL):
            pair_weights(jnp.minimum(trip * UNROLL + part, last), part)

    for part in range(UNROLL):
        slot = (trips - 1) * UNROLL + part
        live = jnp.where(slot < count, 1.0, 0.0).astype(f32)
        add_sums(jnp.clip(slot, 0, last), part, live)

    for copy in copies[3:]:
        copy.wait()
    group = group_of(owners)
    width = group * SLOT

    row = lax.broadcasted_iota(jnp.int32, state_ref.shape, 0)
    still = state_ref[...] + jnp.where(row == 2, -gravity_step, 0.0)
    still = still / jnp.concatenate([inverse_ref[0:1, :]] * 3 + [inverse_ref[1:4, :]], axis=0)

    @pl.loop(0, owners // group)
    def _(block):
        cols = pl.ds(pl.multiple_of(block * width, width), width)
        acc = acc_ref[:, cols]
        place = place_ref[:, cols]
        sphere = sphere_ref[:, cols]
        offset = offset_ref[:, cols]
        total = acc[7:8]
        pull = total * place - acc[0:3]
        press = acc[6:7] * place - acc[8:11]
        scale = press_coef * support_radius
        force = scale * (sphere[6:7] * pull + press) + visc_coef * (acc[3:6] - total * sphere[3:6])
        force = [force[k : k + 1] for k in range(3)]
        turn = cross([offset[k : k + 1] for k in range(3)], force)
        loads = jnp.concatenate(force + turn + [jnp.zeros_like(force[0])] * 2, axis=0)
        high, low = split_two(loads)
        both = jnp.concatenate([high, low], axis=0)
        column = lax.broadcasted_iota(jnp.int32, (clumps, SLOT), 0)
        keep, send = [], []
        for k in range(group):
            here = pl.ds(pl.multiple_of(block * width + k * SLOT, SLOT), SLOT)
            one_hot = jnp.where(column == ids_ref[:, here], 1.0, 0.0).astype(bf16)
            sums = lax.dot_general(
                both[:, k * SLOT : (k + 1) * SLOT], one_hot, (((1,), (1,)), ((), ())),
                preferred_element_type=f32,
            )
            own = jnp.where(block * group + k == me, 1.0, 0.0).astype(f32)
            sums = (sums[0:8] + sums[8:16])[0:6] + own * still
            keep.append(jnp.where(core == 0, sums[0:3], sums[3:6]))
            send.append(jnp.where(core == 0, sums[3:6], sums[0:3]))
        here = pl.ds(pl.multiple_of(block * (3 * group), math.gcd(3 * group, 8)), 3 * group)
        keep_ref[here, :] = jnp.concatenate(keep, axis=0)
        send_ref[here, :] = jnp.concatenate(send, axis=0)


def first_kernel(keep_ref, arrived_ref, inverse_ref, out_ref):
    rows = keep_ref.shape[0]
    out_ref[0:rows, :] = keep_ref[...] + arrived_ref[...]
    linear = jnp.concatenate([inverse_ref[0:1, :]] * 3, axis=0)
    out_ref[rows:, :] = jnp.where(lax.axis_index("sub") == 0, linear, inverse_ref[1:4, :])


def join_kernel(rows, mine_ref, arrived_ref, out_ref):
    more = mine_ref.shape[0] - rows
    out_ref[0:rows, :] = mine_ref[0:rows, :] + arrived_ref[0:rows, :]
    out_ref[rows : rows + more, :] = mine_ref[rows:, :]
    out_ref[rows + more :, :] = arrived_ref[rows:, :]


def update_kernel(partners, mine_ref, arrived_ref, out_ref, inverse_ref):
    owners = len(partners)
    rows = 3 * owners
    half = owners // 2
    me = lax.axis_index("space")
    for k in range(half):
        here = slice(rows + 3 * k, rows + 3 * k + 3)
        inverse_ref[me ^ partners[k]] = mine_ref[here, :]
        inverse_ref[me ^ partners[k + half]] = arrived_ref[here, :]
    totals = mine_ref[0:rows, :] + arrived_ref[0:rows, :]
    out_ref[...] = totals * jnp.concatenate([inverse_ref[k] for k in range(owners)], axis=0)


def velocity_kernel(mine_ref, arrived_ref, offset_ref, ids_ref, clump_ref, sphere_ref, velocity_ref):
    owners, _, clumps = velocity_ref.shape
    group = group_of(owners)
    core = lax.axis_index("sub")

    @pl.loop(0, owners // group)
    def _(block):
        rows = pl.ds(pl.multiple_of(block * (3 * group), math.gcd(3 * group, 8)), 3 * group)
        mine = mine_ref[rows, :]
        arrived = arrived_ref[rows, :]
        linear = jnp.where(core == 0, mine, arrived)
        angular = jnp.where(core == 0, arrived, mine)
        for k in range(group):
            owner = block * group + k
            three = slice(3 * k, 3 * k + 3)
            velocity = jnp.concatenate([linear[three], angular[three]], axis=0)
            velocity_ref[owner] = velocity
            both = jnp.concatenate(
                split_two(jnp.concatenate([velocity, jnp.zeros((2, clumps), f32)], axis=0)), axis=0
            )
            here = pl.ds(pl.multiple_of(owner * SLOT, SLOT), SLOT)
            column = lax.broadcasted_iota(jnp.int32, (clumps, SLOT), 0)
            one_hot = jnp.where(column == ids_ref[:, here], 1.0, 0.0).astype(bf16)
            picked = jnp.dot(both, one_hot, preferred_element_type=f32)
            picked = picked[0:8] + picked[8:16]
            offset = offset_ref[:, here]
            turn = cross([picked[3 + i : 4 + i] for i in range(3)], [offset[i : i + 1] for i in range(3)])
            sphere_ref[:, here] = picked[0:3] + jnp.concatenate(turn, axis=0)

    clump_ref[...] = velocity_ref[lax.axis_index("space")]


def swap(value, axis, bit):
    size = lax.axis_size(axis)
    return lax.ppermute(value, axis, [(k, k ^ bit) for k in range(size)])


def per_device(
    fluid_state, sphere_state, sphere_offset, tile_list, tile_count, clump_ids, clump_state, clump_inverse
):
    owners = lax.axis_size("space")
    spheres = sphere_state.shape[1]
    fluid = fluid_state.shape[1]
    clumps = clump_state.shape[1]
    slots = tile_list.shape[0]
    rows = 3 * owners
    ids = clump_ids.reshape(1, spheres)
    vmem = pl.BlockSpec(memory_space=pltpu.VMEM)
    hbm = pl.BlockSpec(memory_space=pltpu.HBM)
    params = pltpu.CompilerParams(vmem_limit_bytes=48 * 1024 * 1024)

    keep, send = pl.pallas_call(
        loads_kernel,
        out_shape=(pltpu.VMEM((rows, clumps), f32), pltpu.VMEM((rows, clumps), f32)),
        in_specs=[pl.BlockSpec(memory_space=pltpu.SMEM)] + [hbm] * 7,
        out_specs=(vmem, vmem),
        scratch_shapes=[
            pltpu.SMEM((2, slots), jnp.int32),
            pltpu.VMEM((8, fluid), f32),
            pltpu.VMEM((7, spheres), f32),
            pltpu.VMEM((3, spheres), f32),
            pltpu.VMEM((1, spheres), jnp.int32),
            pltpu.VMEM((6, clumps), f32),
            pltpu.VMEM((4, clumps), f32),
            pltpu.SemaphoreType.DMA((7,)),
            pltpu.VMEM((3, spheres), f32),
            pltpu.VMEM((3, fluid, TILE), f32),
            pltpu.VMEM((fluid // TILE, 32, 2 * TILE), bf16),
            pltpu.VMEM((UNROLL, 2 * TILE, TILE), bf16),
            pltpu.VMEM((16, spheres), f32),
        ],
        compiler_params=params,
        name="clump_loads",
    )(tile_count, *(
        pltpu.with_memory_space_constraint(value, pltpu.HBM)
        for value in (
            tile_list.T, fluid_state, sphere_state, sphere_offset, ids, clump_state, clump_inverse
        )
    ))

    def small(kernel, height, name, *operands, scratch=()):
        return pl.pallas_call(
            kernel,
            out_shape=pltpu.VMEM((height, clumps), f32),
            in_specs=[vmem] * len(operands),
            out_specs=vmem,
            scratch_shapes=scratch,
            compiler_params=params,
            name=name,
        )(*operands)

    mine = small(first_kernel, rows + 3, "core_sum", keep, swap(send, "sub", 1), clump_inverse)
    bits = []
    bit = owners // 2
    while bit > 0:
        arrived = swap(mine, "space", bit)
        bits.append(bit)
        if bit > 1:
            height = 2 * mine.shape[0] - rows
            mine = small(functools.partial(join_kernel, rows), height, "space_sum", mine, arrived)
        bit //= 2
    partners = [sum(bit for n, bit in enumerate(bits) if k >> n & 1) for k in range(owners)]
    velocities = small(
        functools.partial(update_kernel, partners), rows, "clump_update", mine, arrived,
        scratch=[pltpu.VMEM((owners, 3, clumps), f32)],
    )

    return pl.pallas_call(
        velocity_kernel,
        out_shape=(
            jax.ShapeDtypeStruct((6, clumps), f32),
            jax.ShapeDtypeStruct((3, spheres), f32),
        ),
        in_specs=[vmem] * 4,
        out_specs=(vmem, vmem),
        scratch_shapes=[pltpu.VMEM((owners, 6, clumps), f32)],
        compiler_params=params,
        name="sphere_velocities",
    )(velocities, swap(velocities, "sub", 1), sphere_offset, ids)


def solution(mesh):
    in_specs = (
        P(None, "space"),
        P(None, "space"),
        P(None, "space"),
        P(("space", "sub"), None),
        P(("space", "sub")),
        P("space"),
        P(None, "space"),
        P(None, "space"),
    )
    out_specs = (P(None, "space"), P(None, "space"))
    return jax.shard_map(
        per_device, mesh=mesh, in_specs=in_specs, out_specs=out_specs, check_vma=False
    )
```

profile of v0, /device:TPU:0, one launch (start us, length us, event | category | flops | bytes accessed | tf_op | source)
XLA Modules:
  0.0 32.1 jit_solution(7597649382032770736)
XLA Ops:
  1.3 10.6 %clump_loads.1 = (f32[48,128]{1,0:T(8,128)S(1)}, f32[48,128]{1,0:T(8,128)S(1)}) custom-call(s32[1]{0:T(128)S(6)} %copy.10.count_ref, s32[2,128]{1,0:T(2,128)} %bitcast.4, f32[8,4096]{1,0:T(8,128)} %fluid_hbm.1, f32[7,4096]{1,0:T(8,128)} %sphere_hbm.1, f32[3,4096]{1,0:T(4,128)} %offset_ref.1, s32[1,4096]{1,0:T(1,128)} %bitcast.2, f32[6,128]{1,0:T(8,128)} %state_hbm.1, ...), custom_call_target="tpu_custom_call" | custom-call | tf_op jit(solution)/shard_map/clump_loads/pallas_call | solution.py:253
  11.9 0.0 copy-start.2
  11.9 0.1 collective-permute-start
  12.0 1.2 %collective-permute-done.arrived_ref = f32[48,128]{1,0:T(8,128)S(1)} collective-permute-done((f32[48,128]{1,0:T(8,128)S(1)}, f32[48,128]{1,0:T(8,128)S(1)}, u32[]{:S(2)}, u32[]{:S(2)}) %collective-permute-start) | collective-permute-done | bytes 24608 | tf_op jit(solution)/shard_map/ppermute | solution.py:236
  13.2 0.0 copy-done.2
  13.2 0.3 collective-permute-start.1
  13.5 4.5 %collective-permute-done.1.arrived_ref = f32[51,128]{1,0:T(8,128)S(1)} collective-permute-done((f32[51,128]{1,0:T(8,128)S(1)}, f32[51,128]{1,0:T(8,128)S(1)}, u32[]{:S(2)}, u32[]{:S(2)}) %collective-permute-start.1) | collective-permute-done | bytes 26144 | tf_op jit(solution)/shard_map/ppermute | solution.py:236
  18.0 0.0 collective-permute-start.2
  18.1 3.9 %collective-permute-done.2.arrived_ref = f32[54,128]{1,0:T(8,128)S(1)} collective-permute-done((f32[54,128]{1,0:T(8,128)S(1)}, f32[54,128]{1,0:T(8,128)S(1)}, u32[]{:S(2)}, u32[]{:S(2)}) %collective-permute-start.2) | collective-permute-done | bytes 27680 | tf_op jit(solution)/shard_map/ppermute | solution.py:236
  21.9 0.7 %collective-permute-start.3 = (f32[60,128]{1,0:T(8,128)S(1)}, f32[60,128]{1,0:T(8,128)S(1)}, u32[]{:S(2)}, u32[]{:S(2)}) collective-permute-start(f32[60,128]{1,0:T(8,128)S(1)} %space_sum.4.mine_ref), channel_id=1, source_target_pairs={{0,4},{2,6},{4,0},{6,2},{8,12},{10,14},{12,8},{14,10},{16,20},{18,... | collective-permute-start | bytes 92168 | tf_op jit(solution)/shard_map/ppermute | solution.py:236
  22.7 3.2 %collective-permute-done.3.arrived_ref = f32[60,128]{1,0:T(8,128)S(1)} collective-permute-done((f32[60,128]{1,0:T(8,128)S(1)}, f32[60,128]{1,0:T(8,128)S(1)}, u32[]{:S(2)}, u32[]{:S(2)}) %collective-permute-start.3) | collective-permute-done | bytes 30752 | tf_op jit(solution)/shard_map/ppermute | solution.py:236
  25.8 0.0 copy-start
  25.8 0.0 copy-start.1
  25.9 0.2 collective-permute-start.4
  26.1 3.8 %collective-permute-done.4.arrived_ref = f32[72,128]{1,0:T(8,128)S(1)} collective-permute-done((f32[72,128]{1,0:T(8,128)S(1)}, f32[72,128]{1,0:T(8,128)S(1)}, u32[]{:S(2)}, u32[]{:S(2)}) %collective-permute-start.4) | collective-permute-done | bytes 36896 | tf_op jit(solution)/shard_map/ppermute | solution.py:236
  29.9 0.1 collective-permute-start.5
  30.0 1.2 %collective-permute-done.5.arrived_ref = f32[48,128]{1,0:T(8,128)S(1)} collective-permute-done((f32[48,128]{1,0:T(8,128)S(1)}, f32[48,128]{1,0:T(8,128)S(1)}, u32[]{:S(2)}, u32[]{:S(2)}) %collective-permute-start.5) | collective-permute-done | bytes 24608 | tf_op jit(solution)/shard_map/ppermute | solution.py:236
  31.2 0.0 copy-done
  31.2 0.0 copy-done.1
  31.2 0.9 %sphere_velocities.1 = (f32[6,128]{1,0:T(8,128)}, f32[3,4096]{1,0:T(4,128)}) custom-call(f32[48,128]{1,0:T(8,128)S(1)} %clump_update.1.mine_ref, f32[48,128]{1,0:T(8,128)S(1)} %collective-permute-done.5.arrived_ref, f32[3,4096]{1,0:T(4,128)S(1)} %copy-done, s32[1,4096]{1,0:T(1,128)S(1)} %bitcast.3), custom_call_target="tpu_custom_call" | custom-call | tf_op jit(solution)/shard_map/sphere_velocities/pallas_call | solution.py:309
  (5 shorter events, 0.0 us)
Async XLA Ops:
  11.9 1.3 %copy-start.2 = (f32[4,128]{1,0:T(4,128)S(1)}, f32[4,128]{1,0:T(4,128)}, u32[]{:S(2)}) copy-start(f32[4,128]{1,0:T(4,128)} %inverse_ref.1) | copy-start | bytes 6148
  11.9 1.3 %collective-permute-start = (f32[48,128]{1,0:T(8,128)S(1)}, f32[48,128]{1,0:T(8,128)S(1)}, u32[]{:S(2)}, u32[]{:S(2)}) collective-permute-start(f32[48,128]{1,0:T(8,128)S(1)} %get-tuple-element.5), channel_id=1, source_target_pairs={{0,1},{1,0},{2,3},{3,2},{4,5},{5,4},{6,7},{7,6},{8,9},{9,8},{10,11... | collective-permute-start | bytes 73736 | tf_op jit(solution)/shard_map/ppermute | solution.py:236
  13.2 4.8 %collective-permute-start.1 = (f32[51,128]{1,0:T(8,128)S(1)}, f32[51,128]{1,0:T(8,128)S(1)}, u32[]{:S(2)}, u32[]{:S(2)}) collective-permute-start(f32[51,128]{1,0:T(8,128)S(1)} %core_sum.1.mine_ref), channel_id=1, source_target_pairs={{0,16},{2,18},{4,20},{6,22},{8,24},{10,26},{12,28},{14,30},{16,0},... | collective-permute-start | bytes 78344 | tf_op jit(solution)/shard_map/ppermute | solution.py:236
  18.0 3.9 %collective-permute-start.2 = (f32[54,128]{1,0:T(8,128)S(1)}, f32[54,128]{1,0:T(8,128)S(1)}, u32[]{:S(2)}, u32[]{:S(2)}) collective-permute-start(f32[54,128]{1,0:T(8,128)S(1)} %space_sum.3.mine_ref), channel_id=1, source_target_pairs={{0,8},{2,10},{4,12},{6,14},{8,0},{10,2},{12,4},{14,6},{16,24},{18,... | collective-permute-start | bytes 82952 | tf_op jit(solution)/shard_map/ppermute | solution.py:236
  21.9 3.9 %collective-permute-start.3 = (f32[60,128]{1,0:T(8,128)S(1)}, f32[60,128]{1,0:T(8,128)S(1)}, u32[]{:S(2)}, u32[]{:S(2)}) collective-permute-start(f32[60,128]{1,0:T(8,128)S(1)} %space_sum.4.mine_ref), channel_id=1, source_target_pairs={{0,4},{2,6},{4,0},{6,2},{8,12},{10,14},{12,8},{14,10},{16,20},{18,... | collective-permute-start | bytes 92168 | tf_op jit(solution)/shard_map/ppermute | solution.py:236
  25.8 5.3 %copy-start = (f32[3,4096]{1,0:T(4,128)S(1)}, f32[3,4096]{1,0:T(4,128)}, u32[]{:S(2)}) copy-start(f32[3,4096]{1,0:T(4,128)} %offset_ref.1) | copy-start | bytes 147460
  25.8 5.3 %copy-start.1 = (s32[4096]{0:T(1024)S(1)}, s32[4096]{0:T(1024)}, u32[]{:S(2)}) copy-start(s32[4096]{0:T(1024)} %param.13) | copy-start | bytes 49156
  25.9 4.0 %collective-permute-start.4 = (f32[72,128]{1,0:T(8,128)S(1)}, f32[72,128]{1,0:T(8,128)S(1)}, u32[]{:S(2)}, u32[]{:S(2)}) collective-permute-start(f32[72,128]{1,0:T(8,128)S(1)} %space_sum.5.mine_ref), channel_id=1, source_target_pairs={{0,2},{2,0},{4,6},{6,4},{8,10},{10,8},{12,14},{14,12},{16,18},{18,... | collective-permute-start | bytes 110600 | tf_op jit(solution)/shard_map/ppermute | solution.py:236
  29.9 1.3 %collective-permute-start.5 = (f32[48,128]{1,0:T(8,128)S(1)}, f32[48,128]{1,0:T(8,128)S(1)}, u32[]{:S(2)}, u32[]{:S(2)}) collective-permute-start(f32[48,128]{1,0:T(8,128)S(1)} %clump_update.1.mine_ref), channel_id=1, source_target_pairs={{0,1},{1,0},{2,3},{3,2},{4,5},{5,4},{6,7},{7,6},{8,9},{9,8},{10,11... | collective-permute-start | bytes 73736 | tf_op jit(solution)/shard_map/ppermute | solution.py:236
where the time goes:
time: 32.4 us; the launch traced here: 32.1 us
  waiting for transfers between devices  17.8 us (55%)
  Pallas kernels  11.6 us (36%)
  starting transfers between devices  1.38 us (4%)
  between operations  1.34 us (4%)
    ppermute x6, waiting for transfers between devices, swap(): return lax.ppermute(value, axis, [(k, k ^ bit) for k in range(size)])  17.8 us
    pallas_call x1, Pallas kernels, per_device(): pl.pallas_call(loads_kernel, out_shape=(pltpu.VMEM((rows, clumps), f32),...  10.6 us
    ppermute x6, starting transfers between devices, swap(): return lax.ppermute(value, axis, [(k, k ^ bit) for k in range(size)])  1.38 us
    pallas_call x1, Pallas kernels, per_device(): pl.pallas_call(velocity_kernel, out_shape=(jax.ShapeDtypeStruct((6, clump...  0.91 us
  transfers between devices with their start and end apart: 6, of which 6 were waited for; matrix products, arithmetic and copies ran while one was open for 0% of the time, Pallas kernels for 0%

commit v1 on v0

--- a/solution.py
+++ b/solution.py
@@ -11,6 +11,8 @@
 TILE = 128
 SLOT = 256
 UNROLL = 8
+LANES = 16
+BLOCK = TILE // LANES
 
 support_radius = 0.5
 press_coef = 4.0
@@ -24,6 +26,12 @@
 def split_two(value):
     high = value.astype(bf16)
     return high, (value - high.astype(f32)).astype(bf16)
+
+
+def split_three(value):
+    high = value.astype(bf16).astype(f32)
+    middle = (value - high).astype(bf16).astype(f32)
+    return high, middle, (value - high) - middle
 
 
 def cross(left, right):
@@ -42,7 +50,7 @@
     count_ref, list_hbm, fluid_hbm, sphere_hbm, offset_hbm, ids_hbm, state_hbm, inverse_hbm,
     keep_ref, send_ref,
     list_ref, fluid_ref, sphere_ref, offset_ref, ids_ref, state_ref, inverse_ref, arrived,
-    place_ref, wide_ref, terms_ref, weight_ref, acc_ref,
+    place_ref, choose_ref, wide_ref, terms_ref, weight_ref, acc_ref,
 ):
     fluid_tiles = fluid_ref.shape[1] // TILE
     clumps = keep_ref.shape[1]
@@ -66,23 +74,33 @@
         copy.start()
 
     acc_ref[...] = jnp.zeros_like(acc_ref)
+
+    lane = lax.broadcasted_iota(jnp.int32, (TILE, 3 * TILE), 0)
+    target = lax.broadcasted_iota(jnp.int32, (TILE, 3 * TILE), 1) // TILE
+    part = lane % LANES
+    wanted = (part == target) | (part == target + 3) | (part == target + 6)
+    for j in range(BLOCK):
+        choose_ref[j] = jnp.where(wanted & (lane // LANES == j), 1.0, 0.0).astype(bf16)
     copies[0].wait()
 
-    @pl.loop(0, fluid_tiles, unroll=8)
-    def _(tile):
-        cols = pl.ds(pl.multiple_of(tile * TILE, TILE), TILE)
-        state = fluid_ref[:, cols]
-        row = lax.broadcasted_iota(jnp.int32, state.shape, 0)
-        state = jnp.where(row < 3, state * (1.0 / support_radius) - 1.0, state)
-        mass = state[7:8]
-        first = jnp.where(row < 7, state * mass, state)
-        second = jnp.where(row < 3, state * (mass * state[6:7]), 0.0)
-        high, low = split_two(jnp.concatenate([first, second], axis=0))
-        both = jnp.concatenate([high, low], axis=0)
-        terms_ref[tile] = jnp.concatenate([both, both], axis=1)
-        turned = state.T
-        for k in range(3):
-            wide_ref[k, cols, :] = jnp.broadcast_to(turned[:, k : k + 1], (TILE, TILE))
+    @pl.loop(0, fluid_tiles // BLOCK)
+    def _(block):
+        row = lax.broadcasted_iota(jnp.int32, (8, TILE), 0)
+        lines = []
+        for j in range(BLOCK):
+            tile = block * BLOCK + j
+            state = fluid_ref[:, pl.ds(pl.multiple_of(tile * TILE, TILE), TILE)]
+            state = jnp.where(row < 3, state * (1.0 / support_radius) - 1.0, state)
+            mass = state[7:8]
+            first = jnp.where(row < 7, state * mass, state)
+            second = jnp.where(row < 3, state * (mass * state[6:7]), 0.0)
+            high, low = split_two(jnp.concatenate([first, second], axis=0))
+            both = jnp.concatenate([high, low], axis=0)
+            terms_ref[tile] = jnp.concatenate([both, both], axis=1)
+            lines += [*split_three(state[0:3]), jnp.zeros((LANES - 9, TILE), f32)]
+        turned = jnp.concatenate(lines, axis=0).T.astype(bf16)
+        for j in range(BLOCK):
+            wide_ref[block * BLOCK + j] = jnp.dot(turned, choose_ref[j], preferred_element_type=f32)
 
     copies[1].wait()
     place_ref[...] = sphere_ref[0:3, :] * (1.0 / support_radius) - 1.0
@@ -92,10 +110,9 @@
         a = list_ref[0, slot]
         b = list_ref[1, slot]
         cols = pl.ds(pl.multiple_of(a * TILE, TILE), TILE)
-        rows = pl.ds(pl.multiple_of(b * TILE, TILE), TILE)
-        dx = place_ref[0:1, cols] - wide_ref[0, rows, :]
-        dy = place_ref[1:2, cols] - wide_ref[1, rows, :]
-        dz = place_ref[2:3, cols] - wide_ref[2, rows, :]
+        dx, dy, dz = [
+            place_ref[k : k + 1, cols] - wide_ref[b, :, k * TILE : (k + 1) * TILE] for k in range(3)
+        ]
         square = jnp.maximum(dx * dx + dy * dy + dz * dz, 1e-30)
         falloff = jnp.maximum(1.0 - square * lax.rsqrt(square), 0.0)
         high, low = split_two(falloff * falloff * falloff)
@@ -179,24 +196,31 @@
     out_ref[rows:, :] = jnp.where(lax.axis_index("sub") == 0, linear, inverse_ref[1:4, :])
 
 
-def join_kernel(rows, mine_ref, arrived_ref, out_ref):
-    more = mine_ref.shape[0] - rows
-    out_ref[0:rows, :] = mine_ref[0:rows, :] + arrived_ref[0:rows, :]
-    out_ref[rows : rows + more, :] = mine_ref[rows:, :]
-    out_ref[rows + more :, :] = arrived_ref[rows:, :]
-
-
-def update_kernel(partners, mine_ref, arrived_ref, out_ref, inverse_ref):
+def sum_rows(refs, rows):
+    sums = [ref[0:rows, :] for ref in refs]
+    while len(sums) > 1:
+        sums = [left + right for left, right in zip(sums[0::2], sums[1::2])]
+    return sums[0]
+
+
+def join_kernel(rows, *refs):
+    *parts, out_ref = refs
+    more = parts[0].shape[0] - rows
+    out_ref[0:rows, :] = sum_rows(parts, rows)
+    for k, ref in enumerate(parts):
+        out_ref[rows + k * more : rows + (k + 1) * more, :] = ref[rows:, :]
+
+
+def update_kernel(partners, *refs):
+    *parts, out_ref, inverse_ref = refs
     owners = len(partners)
     rows = 3 * owners
-    half = owners // 2
+    held = owners // len(parts)
     me = lax.axis_index("space")
-    for k in range(half):
-        here = slice(rows + 3 * k, rows + 3 * k + 3)
-        inverse_ref[me ^ partners[k]] = mine_ref[here, :]
-        inverse_ref[me ^ partners[k + half]] = arrived_ref[here, :]
-    totals = mine_ref[0:rows, :] + arrived_ref[0:rows, :]
-    out_ref[...] = totals * jnp.concatenate([inverse_ref[k] for k in range(owners)], axis=0)
+    for k, partner in enumerate(partners):
+        first = rows + 3 * (k % held)
+        inverse_ref[me ^ partner] = parts[k // held][first : first + 3, :]
+    out_ref[...] = sum_rows(parts, rows) * jnp.concatenate([inverse_ref[k] for k in range(owners)], axis=0)
 
 
 def velocity_kernel(mine_ref, arrived_ref, offset_ref, ids_ref, clump_ref, sphere_ref, velocity_ref):
@@ -265,7 +289,8 @@
             pltpu.VMEM((4, clumps), f32),
             pltpu.SemaphoreType.DMA((7,)),
             pltpu.VMEM((3, spheres), f32),
-            pltpu.VMEM((3, fluid, TILE), f32),
+            pltpu.VMEM((BLOCK, TILE, 3 * TILE), bf16),
+            pltpu.VMEM((fluid // TILE, TILE, 3 * TILE), f32),
             pltpu.VMEM((fluid // TILE, 32, 2 * TILE), bf16),
             pltpu.VMEM((UNROLL, 2 * TILE, TILE), bf16),
             pltpu.VMEM((16, spheres), f32),
@@ -292,17 +317,19 @@
 
     mine = small(first_kernel, rows + 3, "core_sum", keep, swap(send, "sub", 1), clump_inverse)
     bits = []
-    bit = owners // 2
-    while bit > 0:
-        arrived = swap(mine, "space", bit)
-        bits.append(bit)
-        if bit > 1:
-            height = 2 * mine.shape[0] - rows
-            mine = small(functools.partial(join_kernel, rows), height, "space_sum", mine, arrived)
-        bit //= 2
+    left = owners
+    while left > 1:
+        step = [left // 2, left // 4] if left > 2 else [1]
+        left //= 2 ** len(step)
+        bits += step
+        others = step if len(step) == 1 else [*step, sum(step)]
+        parts = [mine] + [swap(mine, "space", bit) for bit in others]
+        if left > 1:
+            height = rows + len(parts) * (mine.shape[0] - rows)
+            mine = small(functools.partial(join_kernel, rows), height, "space_sum", *parts)
     partners = [sum(bit for n, bit in enumerate(bits) if k >> n & 1) for k in range(owners)]
     velocities = small(
-        functools.partial(update_kernel, partners), rows, "clump_update", mine, arrived,
+        functools.partial(update_kernel, partners), rows, "clump_update", *parts,
         scratch=[pltpu.VMEM((owners, 3, clumps), f32)],
     )
 

time: 32.4 us -> 29.1 us (0.90)
  starting transfers between devices: 1.38 us -> 10.7 us
  waiting for transfers between devices: 17.8 us -> 10.3 us
  Pallas kernels: 11.6 us -> 6.62 us
    ppermute x6 -> x8, starting transfers between devices: 1.38 us -> 10.7 us  [swap(): return lax.ppermute(value, axis, [(k, k ^ bit) for k in range(size)])]
    ppermute x6 -> x8, waiting for transfers between devices: 17.8 us -> 10.3 us  [swap(): return lax.ppermute(value, axis, [(k, k ^ bit) for k in range(size)])]
    pallas_call x1, Pallas kernels: 10.6 us -> 5.66 us  [per_device(): pl.pallas_call(loads_kernel, out_shape=(pltpu.VMEM((rows, clumps), f32),...]
  transfers between devices with their start and end apart: 6 -> 8, of which waited for: 6 -> 8; matrix products, arithmetic and copies ran while one was open for 0% -> 0% of each run, Pallas kernels for 0% -> 0%
where the time goes in v1:
time: 29.1 us; the launch traced here: 29 us
  starting transfers between devices  10.7 us (37%)
  waiting for transfers between devices  10.3 us (35%)
  Pallas kernels  6.62 us (23%)
  between operations  1.34 us (5%)
    ppermute x8, starting transfers between devices, swap(): return lax.ppermute(value, axis, [(k, k ^ bit) for k in range(size)])  10.7 us
    ppermute x8, waiting for transfers between devices, swap(): return lax.ppermute(value, axis, [(k, k ^ bit) for k in range(size)])  10.3 us
    pallas_call x1, Pallas kernels, per_device(): pl.pallas_call(loads_kernel, out_shape=(pltpu.VMEM((rows, clumps), f32),...  5.66 us
    pallas_call x1, Pallas kernels, per_device(): pl.pallas_call(velocity_kernel, out_shape=(jax.ShapeDtypeStruct((6, clump...  0.91 us
  transfers between devices with their start and end apart: 8, of which 8 were waited for; matrix products, arithmetic and copies ran while one was open for 0% of the time, Pallas kernels for 0%

profile of v1, /device:TPU:0, one launch (start us, length us, event | category | flops | bytes accessed | tf_op | source)
XLA Modules:
  0.0 29.0 jit_solution(3352841570591741719)
XLA Ops:
  1.3 5.7 %clump_loads.1 = (f32[48,128]{1,0:T(8,128)S(1)}, f32[48,128]{1,0:T(8,128)S(1)}) custom-call(s32[1]{0:T(128)S(6)} %copy.10.count_ref, s32[2,128]{1,0:T(2,128)} %bitcast.4, f32[8,4096]{1,0:T(8,128)} %fluid_hbm.1, f32[7,4096]{1,0:T(8,128)} %sphere_hbm.1, f32[3,4096]{1,0:T(4,128)} %offset_ref.1, s32[1,4096]{1,0:T(1,128)} %bitcast.2, f32[6,128]{1,0:T(8,128)} %state_hbm.1, ...), custom_call_target="tpu_custom_call" | custom-call | tf_op jit(solution)/shard_map/clump_loads/pallas_call | solution.py:277
  6.9 0.0 copy-start.2
  7.0 0.2 collective-permute-start
  7.1 1.1 %collective-permute-done.arrived_ref = f32[48,128]{1,0:T(8,128)S(1)} collective-permute-done((f32[48,128]{1,0:T(8,128)S(1)}, f32[48,128]{1,0:T(8,128)S(1)}, u32[]{:S(2)}, u32[]{:S(2)}) %collective-permute-start) | collective-permute-done | bytes 24608 | tf_op jit(solution)/shard_map/ppermute | solution.py:260
  8.2 0.0 copy-done.2
  8.2 4.6 %collective-permute-start.3 = (f32[51,128]{1,0:T(8,128)S(1)}, f32[51,128]{1,0:T(8,128)S(1)}, u32[]{:S(2)}, u32[]{:S(2)}) collective-permute-start(f32[51,128]{1,0:T(8,128)S(1)} %core_sum.1.refs_0_), channel_id=1, source_target_pairs={{0,24},{2,26},{4,28},{6,30},{8,16},{10,18},{12,20},{14,22},{16,8},... | collective-permute-start | bytes 78344 | tf_op jit(solution)/shard_map/ppermute | solution.py:260
  12.8 0.0 collective-permute-start.2
  12.8 0.6 %collective-permute-start.1 = (f32[51,128]{1,0:T(8,128)S(1)}, f32[51,128]{1,0:T(8,128)S(1)}, u32[]{:S(2)}, u32[]{:S(2)}) collective-permute-start(f32[51,128]{1,0:T(8,128)S(1)} %core_sum.1.refs_0_), channel_id=1, source_target_pairs={{0,16},{2,18},{4,20},{6,22},{8,24},{10,26},{12,28},{14,30},{16,0},... | collective-permute-start | bytes 78344 | tf_op jit(solution)/shard_map/ppermute | solution.py:260
  13.5 1.3 %collective-permute-done.3.refs_3_ = f32[51,128]{1,0:T(8,128)S(1)} collective-permute-done((f32[51,128]{1,0:T(8,128)S(1)}, f32[51,128]{1,0:T(8,128)S(1)}, u32[]{:S(2)}, u32[]{:S(2)}) %collective-permute-start.3) | collective-permute-done | bytes 26144 | tf_op jit(solution)/shard_map/ppermute | solution.py:260
  14.8 2.3 %collective-permute-done.2.refs_2_ = f32[51,128]{1,0:T(8,128)S(1)} collective-permute-done((f32[51,128]{1,0:T(8,128)S(1)}, f32[51,128]{1,0:T(8,128)S(1)}, u32[]{:S(2)}, u32[]{:S(2)}) %collective-permute-start.2) | collective-permute-done | bytes 26144 | tf_op jit(solution)/shard_map/ppermute | solution.py:260
  17.0 0.6 %collective-permute-done.1.refs_1_ = f32[51,128]{1,0:T(8,128)S(1)} collective-permute-done((f32[51,128]{1,0:T(8,128)S(1)}, f32[51,128]{1,0:T(8,128)S(1)}, u32[]{:S(2)}, u32[]{:S(2)}) %collective-permute-start.1) | collective-permute-done | bytes 26144 | tf_op jit(solution)/shard_map/ppermute | solution.py:260
  17.6 0.0 copy-start
  17.6 0.0 copy-start.1
  17.7 4.1 %collective-permute-start.6 = (f32[60,128]{1,0:T(8,128)S(1)}, f32[60,128]{1,0:T(8,128)S(1)}, u32[]{:S(2)}, u32[]{:S(2)}) collective-permute-start(f32[60,128]{1,0:T(8,128)S(1)} %space_sum.1.refs_0_), channel_id=1, source_target_pairs={{0,6},{2,4},{4,2},{6,0},{8,14},{10,12},{12,10},{14,8},{16,22},{18,... | collective-permute-start | bytes 92168 | tf_op jit(solution)/shard_map/ppermute | solution.py:260
  21.7 1.1 %collective-permute-start.5 = (f32[60,128]{1,0:T(8,128)S(1)}, f32[60,128]{1,0:T(8,128)S(1)}, u32[]{:S(2)}, u32[]{:S(2)}) collective-permute-start(f32[60,128]{1,0:T(8,128)S(1)} %space_sum.1.refs_0_), channel_id=1, source_target_pairs={{0,2},{2,0},{4,6},{6,4},{8,10},{10,8},{12,14},{14,12},{16,18},{18,... | collective-permute-start | bytes 92168 | tf_op jit(solution)/shard_map/ppermute | solution.py:260
  22.9 0.0 collective-permute-start.4
  22.9 1.2 %collective-permute-done.6.refs_3_ = f32[60,128]{1,0:T(8,128)S(1)} collective-permute-done((f32[60,128]{1,0:T(8,128)S(1)}, f32[60,128]{1,0:T(8,128)S(1)}, u32[]{:S(2)}, u32[]{:S(2)}) %collective-permute-start.6) | collective-permute-done | bytes 30752 | tf_op jit(solution)/shard_map/ppermute | solution.py:260
  24.1 1.6 %collective-permute-done.5.refs_2_ = f32[60,128]{1,0:T(8,128)S(1)} collective-permute-done((f32[60,128]{1,0:T(8,128)S(1)}, f32[60,128]{1,0:T(8,128)S(1)}, u32[]{:S(2)}, u32[]{:S(2)}) %collective-permute-start.5) | collective-permute-done | bytes 30752 | tf_op jit(solution)/shard_map/ppermute | solution.py:260
  25.7 1.1 %collective-permute-done.4.refs_1_ = f32[60,128]{1,0:T(8,128)S(1)} collective-permute-done((f32[60,128]{1,0:T(8,128)S(1)}, f32[60,128]{1,0:T(8,128)S(1)}, u32[]{:S(2)}, u32[]{:S(2)}) %collective-permute-start.4) | collective-permute-done | bytes 30752 | tf_op jit(solution)/shard_map/ppermute | solution.py:260
  26.8 0.1 collective-permute-start.7
  26.9 1.2 %collective-permute-done.7.arrived_ref = f32[48,128]{1,0:T(8,128)S(1)} collective-permute-done((f32[48,128]{1,0:T(8,128)S(1)}, f32[48,128]{1,0:T(8,128)S(1)}, u32[]{:S(2)}, u32[]{:S(2)}) %collective-permute-start.7) | collective-permute-done | bytes 24608 | tf_op jit(solution)/shard_map/ppermute | solution.py:260
  28.1 0.0 copy-done
  28.1 0.0 copy-done.1
  28.1 0.9 %sphere_velocities.1 = (f32[6,128]{1,0:T(8,128)}, f32[3,4096]{1,0:T(4,128)}) custom-call(f32[48,128]{1,0:T(8,128)S(1)} %clump_update.1.mine_ref, f32[48,128]{1,0:T(8,128)S(1)} %collective-permute-done.7.arrived_ref, f32[3,4096]{1,0:T(4,128)S(1)} %copy-done, s32[1,4096]{1,0:T(1,128)S(1)} %bitcast.3), custom_call_target="tpu_custom_call" | custom-call | tf_op jit(solution)/shard_map/sphere_velocities/pallas_call | solution.py:336
  (3 shorter events, 0.0 us)
Async XLA Ops:
  6.9 1.3 %copy-start.2 = (f32[4,128]{1,0:T(4,128)S(1)}, f32[4,128]{1,0:T(4,128)}, u32[]{:S(2)}) copy-start(f32[4,128]{1,0:T(4,128)} %inverse_ref.1) | copy-start | bytes 6148
  7.0 1.3 %collective-permute-start = (f32[48,128]{1,0:T(8,128)S(1)}, f32[48,128]{1,0:T(8,128)S(1)}, u32[]{:S(2)}, u32[]{:S(2)}) collective-permute-start(f32[48,128]{1,0:T(8,128)S(1)} %get-tuple-element.5), channel_id=1, source_target_pairs={{0,1},{1,0},{2,3},{3,2},{4,5},{5,4},{6,7},{7,6},{8,9},{9,8},{10,11... | collective-permute-start | bytes 73736 | tf_op jit(solution)/shard_map/ppermute | solution.py:260
  8.2 6.5 %collective-permute-start.3 = (f32[51,128]{1,0:T(8,128)S(1)}, f32[51,128]{1,0:T(8,128)S(1)}, u32[]{:S(2)}, u32[]{:S(2)}) collective-permute-start(f32[51,128]{1,0:T(8,128)S(1)} %core_sum.1.refs_0_), channel_id=1, source_target_pairs={{0,24},{2,26},{4,28},{6,30},{8,16},{10,18},{12,20},{14,22},{16,8},... | collective-permute-start | bytes 78344 | tf_op jit(solution)/shard_map/ppermute | solution.py:260
  12.8 4.2 %collective-permute-start.2 = (f32[51,128]{1,0:T(8,128)S(1)}, f32[51,128]{1,0:T(8,128)S(1)}, u32[]{:S(2)}, u32[]{:S(2)}) collective-permute-start(f32[51,128]{1,0:T(8,128)S(1)} %core_sum.1.refs_0_), channel_id=1, source_target_pairs={{0,8},{2,10},{4,12},{6,14},{8,0},{10,2},{12,4},{14,6},{16,24},{18,... | collective-permute-start | bytes 78344 | tf_op jit(solution)/shard_map/ppermute | solution.py:260
  12.8 4.8 %collective-permute-start.1 = (f32[51,128]{1,0:T(8,128)S(1)}, f32[51,128]{1,0:T(8,128)S(1)}, u32[]{:S(2)}, u32[]{:S(2)}) collective-permute-start(f32[51,128]{1,0:T(8,128)S(1)} %core_sum.1.refs_0_), channel_id=1, source_target_pairs={{0,16},{2,18},{4,20},{6,22},{8,24},{10,26},{12,28},{14,30},{16,0},... | collective-permute-start | bytes 78344 | tf_op jit(solution)/shard_map/ppermute | solution.py:260
  17.6 10.5 %copy-start = (f32[3,4096]{1,0:T(4,128)S(1)}, f32[3,4096]{1,0:T(4,128)}, u32[]{:S(2)}) copy-start(f32[3,4096]{1,0:T(4,128)} %offset_ref.1) | copy-start | bytes 147460
  17.6 10.5 %copy-start.1 = (s32[4096]{0:T(1024)S(1)}, s32[4096]{0:T(1024)}, u32[]{:S(2)}) copy-start(s32[4096]{0:T(1024)} %param.13) | copy-start | bytes 49156
  17.7 6.4 %collective-permute-start.6 = (f32[60,128]{1,0:T(8,128)S(1)}, f32[60,128]{1,0:T(8,128)S(1)}, u32[]{:S(2)}, u32[]{:S(2)}) collective-permute-start(f32[60,128]{1,0:T(8,128)S(1)} %space_sum.1.refs_0_), channel_id=1, source_target_pairs={{0,6},{2,4},{4,2},{6,0},{8,14},{10,12},{12,10},{14,8},{16,22},{18,... | collective-permute-start | bytes 92168 | tf_op jit(solution)/shard_map/ppermute | solution.py:260
  21.7 3.9 %collective-permute-start.5 = (f32[60,128]{1,0:T(8,128)S(1)}, f32[60,128]{1,0:T(8,128)S(1)}, u32[]{:S(2)}, u32[]{:S(2)}) collective-permute-start(f32[60,128]{1,0:T(8,128)S(1)} %space_sum.1.refs_0_), channel_id=1, source_target_pairs={{0,2},{2,0},{4,6},{6,4},{8,10},{10,8},{12,14},{14,12},{16,18},{18,... | collective-permute-start | bytes 92168 | tf_op jit(solution)/shard_map/ppermute | solution.py:260
  22.9 3.9 %collective-permute-start.4 = (f32[60,128]{1,0:T(8,128)S(1)}, f32[60,128]{1,0:T(8,128)S(1)}, u32[]{:S(2)}, u32[]{:S(2)}) collective-permute-start(f32[60,128]{1,0:T(8,128)S(1)} %space_sum.1.refs_0_), channel_id=1, source_target_pairs={{0,4},{2,6},{4,0},{6,2},{8,12},{10,14},{12,8},{14,10},{16,20},{18,... | collective-permute-start | bytes 92168 | tf_op jit(solution)/shard_map/ppermute | solution.py:260
  26.8 1.3 %collective-permute-start.7 = (f32[48,128]{1,0:T(8,128)S(1)}, f32[48,128]{1,0:T(8,128)S(1)}, u32[]{:S(2)}, u32[]{:S(2)}) collective-permute-start(f32[48,128]{1,0:T(8,128)S(1)} %clump_update.1.mine_ref), channel_id=1, source_target_pairs={{0,1},{1,0},{2,3},{3,2},{4,5},{5,4},{6,7},{7,6},{8,9},{9,8},{10,11... | collective-permute-start | bytes 73736 | tf_op jit(solution)/shard_map/ppermute | solution.py:260

commit v2 on v1

--- a/solution.py
+++ b/solution.py
@@ -48,15 +48,14 @@
 
 def loads_kernel(
     count_ref, list_hbm, fluid_hbm, sphere_hbm, offset_hbm, ids_hbm, state_hbm, inverse_hbm,
-    keep_ref, send_ref,
+    out_ref,
     list_ref, fluid_ref, sphere_ref, offset_ref, ids_ref, state_ref, inverse_ref, arrived,
     place_ref, choose_ref, wide_ref, terms_ref, weight_ref, acc_ref,
 ):
     fluid_tiles = fluid_ref.shape[1] // TILE
-    clumps = keep_ref.shape[1]
-    owners = keep_ref.shape[0] // 3
-    core = lax.axis_index("sub")
-    me = jnp.where(core == 0, lax.axis_index("space"), -1)
+    clumps = out_ref.shape[1]
+    owners = out_ref.shape[0] // 6
+    me = jnp.where(lax.axis_index("sub") == 0, lax.axis_index("space"), -1)
 
     pairs = (
         (fluid_hbm, fluid_ref),
@@ -172,7 +171,7 @@
         high, low = split_two(loads)
         both = jnp.concatenate([high, low], axis=0)
         column = lax.broadcasted_iota(jnp.int32, (clumps, SLOT), 0)
-        keep, send = [], []
+        results = []
         for k in range(group):
             here = pl.ds(pl.multiple_of(block * width + k * SLOT, SLOT), SLOT)
             one_hot = jnp.where(column == ids_ref[:, here], 1.0, 0.0).astype(bf16)
@@ -181,19 +180,15 @@
                 preferred_element_type=f32,
             )
             own = jnp.where(block * group + k == me, 1.0, 0.0).astype(f32)
-            sums = (sums[0:8] + sums[8:16])[0:6] + own * still
-            keep.append(jnp.where(core == 0, sums[0:3], sums[3:6]))
-            send.append(jnp.where(core == 0, sums[3:6], sums[0:3]))
-        here = pl.ds(pl.multiple_of(block * (3 * group), math.gcd(3 * group, 8)), 3 * group)
-        keep_ref[here, :] = jnp.concatenate(keep, axis=0)
-        send_ref[here, :] = jnp.concatenate(send, axis=0)
-
-
-def first_kernel(keep_ref, arrived_ref, inverse_ref, out_ref):
-    rows = keep_ref.shape[0]
-    out_ref[0:rows, :] = keep_ref[...] + arrived_ref[...]
-    linear = jnp.concatenate([inverse_ref[0:1, :]] * 3, axis=0)
-    out_ref[rows:, :] = jnp.where(lax.axis_index("sub") == 0, linear, inverse_ref[1:4, :])
+            results.append((sums[0:8] + sums[8:16])[0:6] + own * still)
+        here = pl.ds(pl.multiple_of(block * (6 * group), math.gcd(6 * group, 8)), 6 * group)
+        out_ref[here, :] = jnp.concatenate(results, axis=0)
+
+
+def first_kernel(mine_ref, arrived_ref, inverse_ref, out_ref):
+    rows = mine_ref.shape[0]
+    out_ref[0:rows, :] = mine_ref[...] + arrived_ref[...]
+    out_ref[rows:, :] = inverse_ref[...]
 
 
 def sum_rows(refs, rows):
@@ -214,12 +209,13 @@
 def update_kernel(partners, *refs):
     *parts, out_ref, inverse_ref = refs
     owners = len(partners)
-    rows = 3 * owners
+    rows = 6 * owners
     held = owners // len(parts)
     me = lax.axis_index("space")
     for k, partner in enumerate(partners):
-        first = rows + 3 * (k % held)
-        inverse_ref[me ^ partner] = parts[k // held][first : first + 3, :]
+        first = rows + 4 * (k % held)
+        inverse = parts[k // held][first : first + 4, :]
+        inverse_ref[me ^ partner] = jnp.concatenate([inverse[0:1]] * 3 + [inverse[1:4]], axis=0)
     out_ref[...] = sum_rows(parts, rows) * jnp.concatenate([inverse_ref[k] for k in range(owners)], axis=0)
 
 
@@ -230,15 +226,11 @@
 
     @pl.loop(0, owners // group)
     def _(block):
-        rows = pl.ds(pl.multiple_of(block * (3 * group), math.gcd(3 * group, 8)), 3 * group)
-        mine = mine_ref[rows, :]
-        arrived = arrived_ref[rows, :]
-        linear = jnp.where(core == 0, mine, arrived)
-        angular = jnp.where(core == 0, arrived, mine)
+        rows = pl.ds(pl.multiple_of(block * (6 * group), math.gcd(6 * group, 8)), 6 * group)
+        velocities = jnp.where(core == 1, mine_ref[rows, :], arrived_ref[rows, :])
         for k in range(group):
             owner = block * group + k
-            three = slice(3 * k, 3 * k + 3)
-            velocity = jnp.concatenate([linear[three], angular[three]], axis=0)
+            velocity = velocities[6 * k : 6 * k + 6]
             velocity_ref[owner] = velocity
             both = jnp.concatenate(
                 split_two(jnp.concatenate([velocity, jnp.zeros((2, clumps), f32)], axis=0)), axis=0
@@ -255,9 +247,9 @@
     clump_ref[...] = velocity_ref[lax.axis_index("space")]
 
 
-def swap(value, axis, bit):
-    size = lax.axis_size(axis)
-    return lax.ppermute(value, axis, [(k, k ^ bit) for k in range(size)])
+def swap(value, bit):
+    pairs = [(2 * k + 1, 2 * (k ^ bit) + 1) for k in range(lax.axis_size("space"))]
+    return lax.ppermute(value, ("space", "sub"), pairs)
 
 
 def per_device(
@@ -268,17 +260,17 @@
     fluid = fluid_state.shape[1]
     clumps = clump_state.shape[1]
     slots = tile_list.shape[0]
-    rows = 3 * owners
+    rows = 6 * owners
     ids = clump_ids.reshape(1, spheres)
     vmem = pl.BlockSpec(memory_space=pltpu.VMEM)
     hbm = pl.BlockSpec(memory_space=pltpu.HBM)
     params = pltpu.CompilerParams(vmem_limit_bytes=48 * 1024 * 1024)
 
-    keep, send = pl.pallas_call(
+    partial = pl.pallas_call(
         loads_kernel,
-        out_shape=(pltpu.VMEM((rows, clumps), f32), pltpu.VMEM((rows, clumps), f32)),
+        out_shape=pltpu.VMEM((rows, clumps), f32),
         in_specs=[pl.BlockSpec(memory_space=pltpu.SMEM)] + [hbm] * 7,
-        out_specs=(vmem, vmem),
+        out_specs=vmem,
         scratch_shapes=[
             pltpu.SMEM((2, slots), jnp.int32),
             pltpu.VMEM((8, fluid), f32),
@@ -315,7 +307,8 @@
             name=name,
         )(*operands)
 
-    mine = small(first_kernel, rows + 3, "core_sum", keep, swap(send, "sub", 1), clump_inverse)
+    arrived = lax.ppermute(partial, "sub", [(0, 1)])
+    mine = small(first_kernel, rows + 4, "core_sum", partial, arrived, clump_inverse)
     bits = []
     left = owners
     while left > 1:
@@ -323,14 +316,14 @@
         left //= 2 ** len(step)
         bits += step
         others = step if len(step) == 1 else [*step, sum(step)]
-        parts = [mine] + [swap(mine, "space", bit) for bit in others]
+        parts = [mine] + [swap(mine, bit) for bit in others]
         if left > 1:
             height = rows + len(parts) * (mine.shape[0] - rows)
             mine = small(functools.partial(join_kernel, rows), height, "space_sum", *parts)
     partners = [sum(bit for n, bit in enumerate(bits) if k >> n & 1) for k in range(owners)]
     velocities = small(
         functools.partial(update_kernel, partners), rows, "clump_update", *parts,
-        scratch=[pltpu.VMEM((owners, 3, clumps), f32)],
+        scratch=[pltpu.VMEM((owners, 6, clumps), f32)],
     )
 
     return pl.pallas_call(
@@ -344,7 +337,7 @@
         scratch_shapes=[pltpu.VMEM((owners, 6, clumps), f32)],
         compiler_params=params,
         name="sphere_velocities",
-    )(velocities, swap(velocities, "sub", 1), sphere_offset, ids)
+    )(velocities, lax.ppermute(velocities, "sub", [(1, 0)]), sphere_offset, ids)
 
 
 def solution(mesh):

time: 29.1 us -> 40 us (1.37)
  waiting for transfers between devices: 10.3 us -> 23.9 us
  starting transfers between devices: 10.7 us -> 6.98 us
  Pallas kernels: 6.62 us -> 7.42 us
    ppermute x8, waiting for transfers between devices: 10.3 us -> 23.9 us  [the longest x1 23 us: per_device(): lax.ppermute(velocities, 'sub', [(1, 0)])]
    ppermute x8, starting transfers between devices: 10.7 us -> 6.98 us  [the longest x6 4.12 us: swap(): return lax.ppermute(value, ('space', 'sub'), pairs)]
    pallas_call x1, Pallas kernels: 5.66 us -> 6.46 us  [per_device(): pl.pallas_call(loads_kernel, out_shape=pltpu.VMEM((rows, clumps), f32), i...]
  transfers between devices with their start and end apart: 8 -> 8, of which waited for: 8 -> 2; matrix products, arithmetic and copies ran while one was open for 0% -> 0% of each run, Pallas kernels for 0% -> 0%
where the time goes in v2:
time: 40 us; the launch traced here: 39.7 us
  waiting for transfers between devices  23.9 us (60%)
  Pallas kernels  7.42 us (19%)
  starting transfers between devices  6.98 us (17%)
  between operations  1.43 us (4%)
    ppermute x1, waiting for transfers between devices, per_device(): lax.ppermute(velocities, 'sub', [(1, 0)])  23 us
    pallas_call x1, Pallas kernels, per_device(): pl.pallas_call(loads_kernel, out_shape=pltpu.VMEM((rows, clumps), f32), i...  6.46 us
    ppermute x6, starting transfers between devices, swap(): return lax.ppermute(value, ('space', 'sub'), pairs)  4.12 us
    ppermute x1, starting transfers between devices, per_device(): arrived = lax.ppermute(partial, 'sub', [(0, 1)])  1.57 us
    ppermute x1, starting transfers between devices, per_device(): lax.ppermute(velocities, 'sub', [(1, 0)])  1.29 us
    pallas_call x1, Pallas kernels, per_device(): pl.pallas_call(velocity_kernel, out_shape=(jax.ShapeDtypeStruct((6, clump...  0.9 us
    ppermute x1, waiting for transfers between devices, per_device(): arrived = lax.ppermute(partial, 'sub', [(0, 1)])  0.86 us
  transfers between devices with their start and end apart: 8, of which 2 were waited for; matrix products, arithmetic and copies ran while one was open for 0% of the time, Pallas kernels for 0%

profile of v2, /device:TPU:0, one launch (start us, length us, event | category | flops | bytes accessed | tf_op | source)
XLA Modules:
  0.0 39.7 jit_solution(17575239764318742300)
XLA Ops:
  1.3 0.0 copy-start.2
  1.3 6.5 %clump_loads.1.mine_ref = f32[96,128]{1,0:T(8,128)S(1)} custom-call(s32[1]{0:T(128)S(6)} %copy.10.count_ref, s32[2,128]{1,0:T(2,128)} %bitcast.4, f32[8,4096]{1,0:T(8,128)} %fluid_hbm.1, f32[7,4096]{1,0:T(8,128)} %sphere_hbm.1, f32[3,4096]{1,0:T(4,128)} %offset_ref.1, s32[1,4096]{1,0:T(1,128)} %bitcast.2, f32[6,128]{1,0:T(8,128)} %state_hbm.1, ...), custom_call_target="tpu_custom_call" | custom-call | tf_op jit(solution)/shard_map/clump_loads/pallas_call | solution.py:269
  7.8 1.6 %collective-permute-start = (f32[96,128]{1,0:T(8,128)S(1)}, f32[96,128]{1,0:T(8,128)S(1)}, u32[]{:S(2)}, u32[]{:S(2)}) collective-permute-start(f32[96,128]{1,0:T(8,128)S(1)} %clump_loads.1.mine_ref), channel_id=1, source_target_pairs={{0,1},{2,3},{4,5},{6,7},{8,9},{10,11},{12,13},{14,15},{16,17},{18,... | collective-permute-start | bytes 147464 | tf_op jit(solution)/shard_map/ppermute | solution.py:310
  9.3 0.9 %collective-permute-done.arrived_ref = f32[96,128]{1,0:T(8,128)S(1)} collective-permute-done((f32[96,128]{1,0:T(8,128)S(1)}, f32[96,128]{1,0:T(8,128)S(1)}, u32[]{:S(2)}, u32[]{:S(2)}) %collective-permute-start) | collective-permute-done | bytes 49184 | tf_op jit(solution)/shard_map/ppermute | solution.py:310
  10.2 0.0 copy-done.2
  10.2 0.7 %collective-permute-start.3 = (f32[100,128]{1,0:T(8,128)S(1)}, f32[100,128]{1,0:T(8,128)S(1)}, u32[]{:S(2)}, u32[]{:S(2)}) collective-permute-start(f32[100,128]{1,0:T(8,128)S(1)} %core_sum.1.refs_0_), channel_id=1, source_target_pairs={{1,25},{3,27},{5,29},{7,31},{9,17},{11,19},{13,21},{15,23},{17,9},... | collective-permute-start | bytes 153608 | tf_op jit(solution)/shard_map/ppermute | solution.py:252
  10.9 0.7 %collective-permute-start.2 = (f32[100,128]{1,0:T(8,128)S(1)}, f32[100,128]{1,0:T(8,128)S(1)}, u32[]{:S(2)}, u32[]{:S(2)}) collective-permute-start(f32[100,128]{1,0:T(8,128)S(1)} %core_sum.1.refs_0_), channel_id=1, source_target_pairs={{1,9},{3,11},{5,13},{7,15},{9,1},{11,3},{13,5},{15,7},{17,25},{19,... | collective-permute-start | bytes 153608 | tf_op jit(solution)/shard_map/ppermute | solution.py:252
  11.5 0.7 %collective-permute-start.1 = (f32[100,128]{1,0:T(8,128)S(1)}, f32[100,128]{1,0:T(8,128)S(1)}, u32[]{:S(2)}, u32[]{:S(2)}) collective-permute-start(f32[100,128]{1,0:T(8,128)S(1)} %core_sum.1.refs_0_), channel_id=1, source_target_pairs={{1,17},{3,19},{5,21},{7,23},{9,25},{11,27},{13,29},{15,31},{17,1},... | collective-permute-start | bytes 153608 | tf_op jit(solution)/shard_map/ppermute | solution.py:252
  12.2 0.0 collective-permute-done.3.refs_3_
  12.2 0.0 collective-permute-done.2.refs_2_
  12.2 0.0 collective-permute-done.1.refs_1_
  12.3 0.0 copy-start
  12.3 0.0 copy-start.1
  12.3 0.8 %collective-permute-start.6 = (f32[112,128]{1,0:T(8,128)S(1)}, f32[112,128]{1,0:T(8,128)S(1)}, u32[]{:S(2)}, u32[]{:S(2)}) collective-permute-start(f32[112,128]{1,0:T(8,128)S(1)} %space_sum.1.refs_0_), channel_id=1, source_target_pairs={{1,7},{3,5},{5,3},{7,1},{9,15},{11,13},{13,11},{15,9},{17,23},{19,... | collective-permute-start | bytes 172040 | tf_op jit(solution)/shard_map/ppermute | solution.py:252
  13.1 0.7 %collective-permute-start.5 = (f32[112,128]{1,0:T(8,128)S(1)}, f32[112,128]{1,0:T(8,128)S(1)}, u32[]{:S(2)}, u32[]{:S(2)}) collective-permute-start(f32[112,128]{1,0:T(8,128)S(1)} %space_sum.1.refs_0_), channel_id=1, source_target_pairs={{1,3},{3,1},{5,7},{7,5},{9,11},{11,9},{13,15},{15,13},{17,19},{19,... | collective-permute-start | bytes 172040 | tf_op jit(solution)/shard_map/ppermute | solution.py:252
  13.8 0.7 %collective-permute-start.4 = (f32[112,128]{1,0:T(8,128)S(1)}, f32[112,128]{1,0:T(8,128)S(1)}, u32[]{:S(2)}, u32[]{:S(2)}) collective-permute-start(f32[112,128]{1,0:T(8,128)S(1)} %space_sum.1.refs_0_), channel_id=1, source_target_pairs={{1,5},{3,7},{5,1},{7,3},{9,13},{11,15},{13,9},{15,11},{17,21},{19,... | collective-permute-start | bytes 172040 | tf_op jit(solution)/shard_map/ppermute | solution.py:252
  14.4 0.0 collective-permute-done.6.refs_3_
  14.5 0.0 collective-permute-done.5.refs_2_
  14.5 0.0 collective-permute-done.4.refs_1_
  14.5 1.3 %collective-permute-start.7 = (f32[96,128]{1,0:T(8,128)S(1)}, f32[96,128]{1,0:T(8,128)S(1)}, u32[]{:S(2)}, u32[]{:S(2)}) collective-permute-start(f32[96,128]{1,0:T(8,128)S(1)} %clump_update.1.mine_ref), channel_id=1, source_target_pairs={{1,0},{3,2},{5,4},{7,6},{9,8},{11,10},{13,12},{15,14},{17,16},{19,... | collective-permute-start | bytes 147464 | tf_op jit(solution)/shard_map/ppermute | solution.py:340
  15.8 23.0 %collective-permute-done.7.arrived_ref = f32[96,128]{1,0:T(8,128)S(1)} collective-permute-done((f32[96,128]{1,0:T(8,128)S(1)}, f32[96,128]{1,0:T(8,128)S(1)}, u32[]{:S(2)}, u32[]{:S(2)}) %collective-permute-start.7) | collective-permute-done | bytes 49184 | tf_op jit(solution)/shard_map/ppermute | solution.py:340
  38.8 0.0 copy-done
  38.8 0.0 copy-done.1
  38.8 0.9 %sphere_velocities.1 = (f32[6,128]{1,0:T(8,128)}, f32[3,4096]{1,0:T(4,128)}) custom-call(f32[96,128]{1,0:T(8,128)S(1)} %clump_update.1.mine_ref, f32[96,128]{1,0:T(8,128)S(1)} %collective-permute-done.7.arrived_ref, f32[3,4096]{1,0:T(4,128)S(1)} %copy-done, s32[1,4096]{1,0:T(1,128)S(1)} %bitcast.3), custom_call_target="tpu_custom_call" | custom-call | tf_op jit(solution)/shard_map/sphere_velocities/pallas_call | solution.py:329
  (3 shorter events, 0.1 us)
Async XLA Ops:
  1.3 8.9 %copy-start.2 = (f32[4,128]{1,0:T(4,128)S(1)}, f32[4,128]{1,0:T(4,128)}, u32[]{:S(2)}) copy-start(f32[4,128]{1,0:T(4,128)} %inverse_ref.1) | copy-start | bytes 6148
  7.8 2.4 %collective-permute-start = (f32[96,128]{1,0:T(8,128)S(1)}, f32[96,128]{1,0:T(8,128)S(1)}, u32[]{:S(2)}, u32[]{:S(2)}) collective-permute-start(f32[96,128]{1,0:T(8,128)S(1)} %clump_loads.1.mine_ref), channel_id=1, source_target_pairs={{0,1},{2,3},{4,5},{6,7},{8,9},{10,11},{12,13},{14,15},{16,17},{18,... | collective-permute-start | bytes 147464 | tf_op jit(solution)/shard_map/ppermute | solution.py:310
  10.2 2.0 %collective-permute-start.3 = (f32[100,128]{1,0:T(8,128)S(1)}, f32[100,128]{1,0:T(8,128)S(1)}, u32[]{:S(2)}, u32[]{:S(2)}) collective-permute-start(f32[100,128]{1,0:T(8,128)S(1)} %core_sum.1.refs_0_), channel_id=1, source_target_pairs={{1,25},{3,27},{5,29},{7,31},{9,17},{11,19},{13,21},{15,23},{17,9},... | collective-permute-start | bytes 153608 | tf_op jit(solution)/shard_map/ppermute | solution.py:252
  10.9 1.4 %collective-permute-start.2 = (f32[100,128]{1,0:T(8,128)S(1)}, f32[100,128]{1,0:T(8,128)S(1)}, u32[]{:S(2)}, u32[]{:S(2)}) collective-permute-start(f32[100,128]{1,0:T(8,128)S(1)} %core_sum.1.refs_0_), channel_id=1, source_target_pairs={{1,9},{3,11},{5,13},{7,15},{9,1},{11,3},{13,5},{15,7},{17,25},{19,... | collective-permute-start | bytes 153608 | tf_op jit(solution)/shard_map/ppermute | solution.py:252
  11.5 0.7 %collective-permute-start.1 = (f32[100,128]{1,0:T(8,128)S(1)}, f32[100,128]{1,0:T(8,128)S(1)}, u32[]{:S(2)}, u32[]{:S(2)}) collective-permute-start(f32[100,128]{1,0:T(8,128)S(1)} %core_sum.1.refs_0_), channel_id=1, source_target_pairs={{1,17},{3,19},{5,21},{7,23},{9,25},{11,27},{13,29},{15,31},{17,1},... | collective-permute-start | bytes 153608 | tf_op jit(solution)/shard_map/ppermute | solution.py:252
  12.3 26.5 %copy-start = (f32[3,4096]{1,0:T(4,128)S(1)}, f32[3,4096]{1,0:T(4,128)}, u32[]{:S(2)}) copy-start(f32[3,4096]{1,0:T(4,128)} %offset_ref.1) | copy-start | bytes 147460
  12.3 26.5 %copy-start.1 = (s32[4096]{0:T(1024)S(1)}, s32[4096]{0:T(1024)}, u32[]{:S(2)}) copy-start(s32[4096]{0:T(1024)} %param.13) | copy-start | bytes 49156
  12.3 2.2 %collective-permute-start.6 = (f32[112,128]{1,0:T(8,128)S(1)}, f32[112,128]{1,0:T(8,128)S(1)}, u32[]{:S(2)}, u32[]{:S(2)}) collective-permute-start(f32[112,128]{1,0:T(8,128)S(1)} %space_sum.1.refs_0_), channel_id=1, source_target_pairs={{1,7},{3,5},{5,3},{7,1},{9,15},{11,13},{13,11},{15,9},{17,23},{19,... | collective-permute-start | bytes 172040 | tf_op jit(solution)/shard_map/ppermute | solution.py:252
  13.1 1.4 %collective-permute-start.5 = (f32[112,128]{1,0:T(8,128)S(1)}, f32[112,128]{1,0:T(8,128)S(1)}, u32[]{:S(2)}, u32[]{:S(2)}) collective-permute-start(f32[112,128]{1,0:T(8,128)S(1)} %space_sum.1.refs_0_), channel_id=1, source_target_pairs={{1,3},{3,1},{5,7},{7,5},{9,11},{11,9},{13,15},{15,13},{17,19},{19,... | collective-permute-start | bytes 172040 | tf_op jit(solution)/shard_map/ppermute | solution.py:252
  13.8 0.7 %collective-permute-start.4 = (f32[112,128]{1,0:T(8,128)S(1)}, f32[112,128]{1,0:T(8,128)S(1)}, u32[]{:S(2)}, u32[]{:S(2)}) collective-permute-start(f32[112,128]{1,0:T(8,128)S(1)} %space_sum.1.refs_0_), channel_id=1, source_target_pairs={{1,5},{3,7},{5,1},{7,3},{9,13},{11,15},{13,9},{15,11},{17,21},{19,... | collective-permute-start | bytes 172040 | tf_op jit(solution)/shard_map/ppermute | solution.py:252
  14.5 24.3 %collective-permute-start.7 = (f32[96,128]{1,0:T(8,128)S(1)}, f32[96,128]{1,0:T(8,128)S(1)}, u32[]{:S(2)}, u32[]{:S(2)}) collective-permute-start(f32[96,128]{1,0:T(8,128)S(1)} %clump_update.1.mine_ref), channel_id=1, source_target_pairs={{1,0},{3,2},{5,4},{7,6},{9,8},{11,10},{13,12},{15,14},{17,16},{19,... | collective-permute-start | bytes 147464 | tf_op jit(solution)/shard_map/ppermute | solution.py:340

commit v3 on v2

--- a/solution.py
+++ b/solution.py
@@ -248,7 +248,8 @@
 
 
 def swap(value, bit):
-    pairs = [(2 * k + 1, 2 * (k ^ bit) + 1) for k in range(lax.axis_size("space"))]
+    chips = range(lax.axis_size("space"))
+    pairs = [(2 * k, 2 * k) for k in chips] + [(2 * k + 1, 2 * (k ^ bit) + 1) for k in chips]
     return lax.ppermute(value, ("space", "sub"), pairs)
 
 
@@ -307,7 +308,7 @@
             name=name,
         )(*operands)
 
-    arrived = lax.ppermute(partial, "sub", [(0, 1)])
+    arrived = lax.ppermute(partial, "sub", [(0, 1), (1, 0)])
     mine = small(first_kernel, rows + 4, "core_sum", partial, arrived, clump_inverse)
     bits = []
     left = owners
@@ -337,7 +338,7 @@
         scratch_shapes=[pltpu.VMEM((owners, 6, clumps), f32)],
         compiler_params=params,
         name="sphere_velocities",
-    )(velocities, lax.ppermute(velocities, "sub", [(1, 0)]), sphere_offset, ids)
+    )(velocities, lax.ppermute(velocities, "sub", [(0, 1), (1, 0)]), sphere_offset, ids)
 
 
 def solution(mesh):

time: 40 us -> 38.7 us (0.968)
  waiting for transfers between devices: 23.9 us -> 1.78 us
  starting transfers between devices: 6.98 us -> 28.5 us
  Pallas kernels: 7.42 us -> 6.66 us
    ppermute x2, waiting for transfers between devices: 23.9 us -> 1.76 us  [the longest x1 0.88 us: per_device(): arrived = lax.ppermute(partial, 'sub', [(0, 1), (1, 0)])]
    ppermute x2, starting transfers between devices: 2.86 us -> 24.4 us  [the longest x1 23.9 us: per_device(): lax.ppermute(velocities, 'sub', [(0, 1), (1, 0)])]
    pallas_call x1, Pallas kernels: 6.46 us -> 5.69 us  [per_device(): pl.pallas_call(loads_kernel, out_shape=pltpu.VMEM((rows, clumps), f32), i...]
where the time goes in v3:
time: 38.7 us; the launch traced here: 38.4 us
  starting transfers between devices  28.5 us (74%)
  Pallas kernels  6.66 us (17%)
  waiting for transfers between devices  1.78 us (5%)
  between operations  1.42 us (4%)
    ppermute x1, starting transfers between devices, per_device(): lax.ppermute(velocities, 'sub', [(0, 1), (1, 0)])  23.9 us
    pallas_call x1, Pallas kernels, per_device(): pl.pallas_call(loads_kernel, out_shape=pltpu.VMEM((rows, clumps), f32), i...  5.69 us
    ppermute x6, starting transfers between devices, swap(): return lax.ppermute(value, ('space', 'sub'), pairs)  4.12 us
    pallas_call x1, Pallas kernels, per_device(): pl.pallas_call(velocity_kernel, out_shape=(jax.ShapeDtypeStruct((6, clump...  0.9 us
    ppermute x1, waiting for transfers between devices, per_device(): arrived = lax.ppermute(partial, 'sub', [(0, 1), (1, 0)])  0.88 us
    ppermute x1, waiting for transfers between devices, per_device(): lax.ppermute(velocities, 'sub', [(0, 1), (1, 0)])  0.88 us
  transfers between devices with their start and end apart: 8, of which 2 were waited for; matrix products, arithmetic and copies ran while one was open for 0% of the time, Pallas kernels for 0%

profile of v3, /device:TPU:0, one launch (start us, length us, event | category | flops | bytes accessed | tf_op | source)
XLA Modules:
  0.0 38.4 jit_solution(9924214887508467825)
XLA Ops:
  1.3 0.0 copy-start.2
  1.3 5.7 %clump_loads.1.mine_ref = f32[96,128]{1,0:T(8,128)S(1)} custom-call(s32[1]{0:T(128)S(6)} %copy.10.count_ref, s32[2,128]{1,0:T(2,128)} %bitcast.4, f32[8,4096]{1,0:T(8,128)} %fluid_hbm.1, f32[7,4096]{1,0:T(8,128)} %sphere_hbm.1, f32[3,4096]{1,0:T(4,128)} %offset_ref.1, s32[1,4096]{1,0:T(1,128)} %bitcast.2, f32[6,128]{1,0:T(8,128)} %state_hbm.1, ...), custom_call_target="tpu_custom_call" | custom-call | tf_op jit(solution)/shard_map/clump_loads/pallas_call | solution.py:270
  7.0 0.5 %collective-permute-start = (f32[96,128]{1,0:T(8,128)S(1)}, f32[96,128]{1,0:T(8,128)S(1)}, u32[]{:S(2)}, u32[]{:S(2)}) collective-permute-start(f32[96,128]{1,0:T(8,128)S(1)} %clump_loads.1.mine_ref), channel_id=1, source_target_pairs={{0,1},{1,0},{2,3},{3,2},{4,5},{5,4},{6,7},{7,6},{8,9},{9,8},{10,11... | collective-permute-start | bytes 147464 | tf_op jit(solution)/shard_map/ppermute | solution.py:311
  7.5 0.9 %collective-permute-done.arrived_ref = f32[96,128]{1,0:T(8,128)S(1)} collective-permute-done((f32[96,128]{1,0:T(8,128)S(1)}, f32[96,128]{1,0:T(8,128)S(1)}, u32[]{:S(2)}, u32[]{:S(2)}) %collective-permute-start) | collective-permute-done | bytes 49184 | tf_op jit(solution)/shard_map/ppermute | solution.py:311
  8.4 0.0 copy-done.2
  8.4 0.7 %collective-permute-start.3 = (f32[100,128]{1,0:T(8,128)S(1)}, f32[100,128]{1,0:T(8,128)S(1)}, u32[]{:S(2)}, u32[]{:S(2)}) collective-permute-start(f32[100,128]{1,0:T(8,128)S(1)} %core_sum.1.refs_0_), channel_id=1, source_target_pairs={{0,0},{2,2},{4,4},{6,6},{8,8},{10,10},{12,12},{14,14},{16,16},{18,... | collective-permute-start | bytes 153608 | tf_op jit(solution)/shard_map/ppermute | solution.py:253
  9.0 0.7 %collective-permute-start.2 = (f32[100,128]{1,0:T(8,128)S(1)}, f32[100,128]{1,0:T(8,128)S(1)}, u32[]{:S(2)}, u32[]{:S(2)}) collective-permute-start(f32[100,128]{1,0:T(8,128)S(1)} %core_sum.1.refs_0_), channel_id=1, source_target_pairs={{0,0},{2,2},{4,4},{6,6},{8,8},{10,10},{12,12},{14,14},{16,16},{18,... | collective-permute-start | bytes 153608 | tf_op jit(solution)/shard_map/ppermute | solution.py:253
  9.7 0.7 %collective-permute-start.1 = (f32[100,128]{1,0:T(8,128)S(1)}, f32[100,128]{1,0:T(8,128)S(1)}, u32[]{:S(2)}, u32[]{:S(2)}) collective-permute-start(f32[100,128]{1,0:T(8,128)S(1)} %core_sum.1.refs_0_), channel_id=1, source_target_pairs={{0,0},{2,2},{4,4},{6,6},{8,8},{10,10},{12,12},{14,14},{16,16},{18,... | collective-permute-start | bytes 153608 | tf_op jit(solution)/shard_map/ppermute | solution.py:253
  10.4 0.0 collective-permute-done.3.refs_3_
  10.4 0.0 collective-permute-done.2.refs_2_
  10.4 0.0 collective-permute-done.1.refs_1_
  10.4 0.0 copy-start
  10.5 0.0 copy-start.1
  10.5 0.8 %collective-permute-start.6 = (f32[112,128]{1,0:T(8,128)S(1)}, f32[112,128]{1,0:T(8,128)S(1)}, u32[]{:S(2)}, u32[]{:S(2)}) collective-permute-start(f32[112,128]{1,0:T(8,128)S(1)} %space_sum.1.refs_0_), channel_id=1, source_target_pairs={{0,0},{2,2},{4,4},{6,6},{8,8},{10,10},{12,12},{14,14},{16,16},{18,... | collective-permute-start | bytes 172040 | tf_op jit(solution)/shard_map/ppermute | solution.py:253
  11.3 0.7 %collective-permute-start.5 = (f32[112,128]{1,0:T(8,128)S(1)}, f32[112,128]{1,0:T(8,128)S(1)}, u32[]{:S(2)}, u32[]{:S(2)}) collective-permute-start(f32[112,128]{1,0:T(8,128)S(1)} %space_sum.1.refs_0_), channel_id=1, source_target_pairs={{0,0},{2,2},{4,4},{6,6},{8,8},{10,10},{12,12},{14,14},{16,16},{18,... | collective-permute-start | bytes 172040 | tf_op jit(solution)/shard_map/ppermute | solution.py:253
  11.9 0.7 %collective-permute-start.4 = (f32[112,128]{1,0:T(8,128)S(1)}, f32[112,128]{1,0:T(8,128)S(1)}, u32[]{:S(2)}, u32[]{:S(2)}) collective-permute-start(f32[112,128]{1,0:T(8,128)S(1)} %space_sum.1.refs_0_), channel_id=1, source_target_pairs={{0,0},{2,2},{4,4},{6,6},{8,8},{10,10},{12,12},{14,14},{16,16},{18,... | collective-permute-start | bytes 172040 | tf_op jit(solution)/shard_map/ppermute | solution.py:253
  12.6 0.0 collective-permute-done.6.refs_3_
  12.6 0.0 collective-permute-done.5.refs_2_
  12.6 0.0 collective-permute-done.4.refs_1_
  12.7 23.9 %collective-permute-start.7 = (f32[96,128]{1,0:T(8,128)S(1)}, f32[96,128]{1,0:T(8,128)S(1)}, u32[]{:S(2)}, u32[]{:S(2)}) collective-permute-start(f32[96,128]{1,0:T(8,128)S(1)} %clump_update.1.mine_ref), channel_id=1, source_target_pairs={{0,1},{1,0},{2,3},{3,2},{4,5},{5,4},{6,7},{7,6},{8,9},{9,8},{10,11... | collective-permute-start | bytes 147464 | tf_op jit(solution)/shard_map/ppermute | solution.py:341
  36.6 0.9 %collective-permute-done.7.arrived_ref = f32[96,128]{1,0:T(8,128)S(1)} collective-permute-done((f32[96,128]{1,0:T(8,128)S(1)}, f32[96,128]{1,0:T(8,128)S(1)}, u32[]{:S(2)}, u32[]{:S(2)}) %collective-permute-start.7) | collective-permute-done | bytes 49184 | tf_op jit(solution)/shard_map/ppermute | solution.py:341
  37.4 0.0 copy-done
  37.4 0.0 copy-done.1
  37.4 0.9 %sphere_velocities.1 = (f32[6,128]{1,0:T(8,128)}, f32[3,4096]{1,0:T(4,128)}) custom-call(f32[96,128]{1,0:T(8,128)S(1)} %clump_update.1.mine_ref, f32[96,128]{1,0:T(8,128)S(1)} %collective-permute-done.7.arrived_ref, f32[3,4096]{1,0:T(4,128)S(1)} %copy-done, s32[1,4096]{1,0:T(1,128)S(1)} %bitcast.3), custom_call_target="tpu_custom_call" | custom-call | tf_op jit(solution)/shard_map/sphere_velocities/pallas_call | solution.py:330
  (3 shorter events, 0.1 us)
Async XLA Ops:
  1.3 7.1 %copy-start.2 = (f32[4,128]{1,0:T(4,128)S(1)}, f32[4,128]{1,0:T(4,128)}, u32[]{:S(2)}) copy-start(f32[4,128]{1,0:T(4,128)} %inverse_ref.1) | copy-start | bytes 6148
  7.0 1.4 %collective-permute-start = (f32[96,128]{1,0:T(8,128)S(1)}, f32[96,128]{1,0:T(8,128)S(1)}, u32[]{:S(2)}, u32[]{:S(2)}) collective-permute-start(f32[96,128]{1,0:T(8,128)S(1)} %clump_loads.1.mine_ref), channel_id=1, source_target_pairs={{0,1},{1,0},{2,3},{3,2},{4,5},{5,4},{6,7},{7,6},{8,9},{9,8},{10,11... | collective-permute-start | bytes 147464 | tf_op jit(solution)/shard_map/ppermute | solution.py:311
  8.4 2.0 %collective-permute-start.3 = (f32[100,128]{1,0:T(8,128)S(1)}, f32[100,128]{1,0:T(8,128)S(1)}, u32[]{:S(2)}, u32[]{:S(2)}) collective-permute-start(f32[100,128]{1,0:T(8,128)S(1)} %core_sum.1.refs_0_), channel_id=1, source_target_pairs={{0,0},{2,2},{4,4},{6,6},{8,8},{10,10},{12,12},{14,14},{16,16},{18,... | collective-permute-start | bytes 153608 | tf_op jit(solution)/shard_map/ppermute | solution.py:253
  9.0 1.4 %collective-permute-start.2 = (f32[100,128]{1,0:T(8,128)S(1)}, f32[100,128]{1,0:T(8,128)S(1)}, u32[]{:S(2)}, u32[]{:S(2)}) collective-permute-start(f32[100,128]{1,0:T(8,128)S(1)} %core_sum.1.refs_0_), channel_id=1, source_target_pairs={{0,0},{2,2},{4,4},{6,6},{8,8},{10,10},{12,12},{14,14},{16,16},{18,... | collective-permute-start | bytes 153608 | tf_op jit(solution)/shard_map/ppermute | solution.py:253
  9.7 0.7 %collective-permute-start.1 = (f32[100,128]{1,0:T(8,128)S(1)}, f32[100,128]{1,0:T(8,128)S(1)}, u32[]{:S(2)}, u32[]{:S(2)}) collective-permute-start(f32[100,128]{1,0:T(8,128)S(1)} %core_sum.1.refs_0_), channel_id=1, source_target_pairs={{0,0},{2,2},{4,4},{6,6},{8,8},{10,10},{12,12},{14,14},{16,16},{18,... | collective-permute-start | bytes 153608 | tf_op jit(solution)/shard_map/ppermute | solution.py:253
  10.4 27.0 %copy-start = (f32[3,4096]{1,0:T(4,128)S(1)}, f32[3,4096]{1,0:T(4,128)}, u32[]{:S(2)}) copy-start(f32[3,4096]{1,0:T(4,128)} %offset_ref.1) | copy-start | bytes 147460
  10.5 27.0 %copy-start.1 = (s32[4096]{0:T(1024)S(1)}, s32[4096]{0:T(1024)}, u32[]{:S(2)}) copy-start(s32[4096]{0:T(1024)} %param.13) | copy-start | bytes 49156
  10.5 2.2 %collective-permute-start.6 = (f32[112,128]{1,0:T(8,128)S(1)}, f32[112,128]{1,0:T(8,128)S(1)}, u32[]{:S(2)}, u32[]{:S(2)}) collective-permute-start(f32[112,128]{1,0:T(8,128)S(1)} %space_sum.1.refs_0_), channel_id=1, source_target_pairs={{0,0},{2,2},{4,4},{6,6},{8,8},{10,10},{12,12},{14,14},{16,16},{18,... | collective-permute-start | bytes 172040 | tf_op jit(solution)/shard_map/ppermute | solution.py:253
  11.3 1.4 %collective-permute-start.5 = (f32[112,128]{1,0:T(8,128)S(1)}, f32[112,128]{1,0:T(8,128)S(1)}, u32[]{:S(2)}, u32[]{:S(2)}) collective-permute-start(f32[112,128]{1,0:T(8,128)S(1)} %space_sum.1.refs_0_), channel_id=1, source_target_pairs={{0,0},{2,2},{4,4},{6,6},{8,8},{10,10},{12,12},{14,14},{16,16},{18,... | collective-permute-start | bytes 172040 | tf_op jit(solution)/shard_map/ppermute | solution.py:253
  11.9 0.7 %collective-permute-start.4 = (f32[112,128]{1,0:T(8,128)S(1)}, f32[112,128]{1,0:T(8,128)S(1)}, u32[]{:S(2)}, u32[]{:S(2)}) collective-permute-start(f32[112,128]{1,0:T(8,128)S(1)} %space_sum.1.refs_0_), channel_id=1, source_target_pairs={{0,0},{2,2},{4,4},{6,6},{8,8},{10,10},{12,12},{14,14},{16,16},{18,... | collective-permute-start | bytes 172040 | tf_op jit(solution)/shard_map/ppermute | solution.py:253
  12.7 24.8 %collective-permute-start.7 = (f32[96,128]{1,0:T(8,128)S(1)}, f32[96,128]{1,0:T(8,128)S(1)}, u32[]{:S(2)}, u32[]{:S(2)}) collective-permute-start(f32[96,128]{1,0:T(8,128)S(1)} %clump_update.1.mine_ref), channel_id=1, source_target_pairs={{0,1},{1,0},{2,3},{3,2},{4,5},{5,4},{6,7},{7,6},{8,9},{9,8},{10,11... | collective-permute-start | bytes 147464 | tf_op jit(solution)/shard_map/ppermute | solution.py:341

commit v4 on v1

--- a/solution.py
+++ b/solution.py
@@ -196,30 +196,26 @@
     out_ref[rows:, :] = jnp.where(lax.axis_index("sub") == 0, linear, inverse_ref[1:4, :])
 
 
-def sum_rows(refs, rows):
-    sums = [ref[0:rows, :] for ref in refs]
-    while len(sums) > 1:
-        sums = [left + right for left, right in zip(sums[0::2], sums[1::2])]
-    return sums[0]
-
-
-def join_kernel(rows, *refs):
-    *parts, out_ref = refs
-    more = parts[0].shape[0] - rows
+def sum_rows(parts, rows):
+    return functools.reduce(lambda total, part: total + part, [part[0:rows, :] for part in parts])
+
+
+def join_kernel(rows, parts_ref, out_ref):
+    parts = [parts_ref.at[k] for k in range(parts_ref.shape[0])]
+    more = parts_ref.shape[1] - rows
     out_ref[0:rows, :] = sum_rows(parts, rows)
-    for k, ref in enumerate(parts):
-        out_ref[rows + k * more : rows + (k + 1) * more, :] = ref[rows:, :]
-
-
-def update_kernel(partners, *refs):
-    *parts, out_ref, inverse_ref = refs
-    owners = len(partners)
+    for k, part in enumerate(parts):
+        out_ref[rows + k * more : rows + (k + 1) * more, :] = part[rows:, :]
+
+
+def update_kernel(holders, parts_ref, out_ref, inverse_ref):
+    parts = [parts_ref.at[k] for k in range(parts_ref.shape[0])]
+    owners = len(holders)
     rows = 3 * owners
     held = owners // len(parts)
-    me = lax.axis_index("space")
-    for k, partner in enumerate(partners):
+    for k, owner in enumerate(holders):
         first = rows + 3 * (k % held)
-        inverse_ref[me ^ partner] = parts[k // held][first : first + 3, :]
+        inverse_ref[owner] = parts[k // held][first : first + 3, :]
     out_ref[...] = sum_rows(parts, rows) * jnp.concatenate([inverse_ref[k] for k in range(owners)], axis=0)
 
 
@@ -316,20 +312,23 @@
         )(*operands)
 
     mine = small(first_kernel, rows + 3, "core_sum", keep, swap(send, "sub", 1), clump_inverse)
-    bits = []
-    left = owners
-    while left > 1:
-        step = [left // 2, left // 4] if left > 2 else [1]
-        left //= 2 ** len(step)
-        bits += step
-        others = step if len(step) == 1 else [*step, sum(step)]
-        parts = [mine] + [swap(mine, "space", bit) for bit in others]
-        if left > 1:
-            height = rows + len(parts) * (mine.shape[0] - rows)
-            mine = small(functools.partial(join_kernel, rows), height, "space_sum", *parts)
-    partners = [sum(bit for n, bit in enumerate(bits) if k >> n & 1) for k in range(owners)]
+    holders = [0]
+    stride = owners
+    while stride > 1:
+        count = math.gcd(stride, 4)
+        stride //= count
+        groups = [
+            [first + k * stride for k in range(count)]
+            for first in range(owners)
+            if first // stride % count == 0
+        ]
+        parts = lax.all_gather(mine, "space", axis_index_groups=groups)
+        holders = [owner + k * stride for k in range(count) for owner in holders]
+        if stride > 1:
+            height = rows + count * (mine.shape[0] - rows)
+            mine = small(functools.partial(join_kernel, rows), height, "space_sum", parts)
     velocities = small(
-        functools.partial(update_kernel, partners), rows, "clump_update", *parts,
+        functools.partial(update_kernel, holders), rows, "clump_update", parts,
         scratch=[pltpu.VMEM((owners, 3, clumps), f32)],
     )
 

time: 29.1 us -> 36.3 us (1.25)
  blocking collectives: 0 us -> 25.8 us
  starting transfers between devices: 10.7 us -> 0.24 us
  waiting for transfers between devices: 10.3 us -> 2.27 us
    all_gather x0 -> x2, blocking collectives: none -> 25.8 us  [per_device(): parts = lax.all_gather(mine, 'space', axis_index_groups=groups)]
    ppermute x8 -> x2, starting transfers between devices: 10.7 us -> 0.24 us  [swap(): return lax.ppermute(value, axis, [(k, k ^ bit) for k in range(size)])]
    ppermute x8 -> x2, waiting for transfers between devices: 10.3 us -> 2.27 us  [swap(): return lax.ppermute(value, axis, [(k, k ^ bit) for k in range(size)])]
  transfers between devices with their start and end apart: 8 -> 2, of which waited for: 8 -> 2; matrix products, arithmetic and copies ran while one was open for 0% -> 0% of each run, Pallas kernels for 0% -> 0%
where the time goes in v4:
time: 36.3 us; the launch traced here: 36.2 us
  blocking collectives  25.8 us (71%)
  Pallas kernels  6.6 us (18%)
  waiting for transfers between devices  2.27 us (6%)
  between operations  1.32 us (4%)
    all_gather x2, blocking collectives, per_device(): parts = lax.all_gather(mine, 'space', axis_index_groups=groups)  25.8 us
    pallas_call x1, Pallas kernels, per_device(): pl.pallas_call(loads_kernel, out_shape=(pltpu.VMEM((rows, clumps), f32),...  5.66 us
    ppermute x2, waiting for transfers between devices, swap(): return lax.ppermute(value, axis, [(k, k ^ bit) for k in range(size)])  2.27 us
    pallas_call x1, Pallas kernels, per_device(): pl.pallas_call(velocity_kernel, out_shape=(jax.ShapeDtypeStruct((6, clump...  0.91 us
  transfers between devices with their start and end apart: 2, of which 2 were waited for; matrix products, arithmetic and copies ran while one was open for 0% of the time, Pallas kernels for 0%

profile of v4, /device:TPU:0, one launch (start us, length us, event | category | flops | bytes accessed | tf_op | source)
XLA Modules:
  0.0 36.2 jit_solution(5489602841291566789)
XLA Ops:
  1.3 5.7 %clump_loads.1 = (f32[48,128]{1,0:T(8,128)S(1)}, f32[48,128]{1,0:T(8,128)S(1)}) custom-call(s32[1]{0:T(128)S(6)} %copy.10.count_ref, s32[2,128]{1,0:T(2,128)} %bitcast.8, f32[8,4096]{1,0:T(8,128)} %fluid_hbm.1, f32[7,4096]{1,0:T(8,128)} %sphere_hbm.1, f32[3,4096]{1,0:T(4,128)} %offset_ref.1, s32[1,4096]{1,0:T(1,128)} %bitcast.6, f32[6,128]{1,0:T(8,128)} %state_hbm.1, ...), custom_call_target="tpu_custom_call" | custom-call | tf_op jit(solution)/shard_map/clump_loads/pallas_call | solution.py:273
  6.9 0.0 copy-start.2
  7.0 0.2 collective-permute-start
  7.1 1.1 %collective-permute-done.arrived_ref = f32[48,128]{1,0:T(8,128)S(1)} collective-permute-done((f32[48,128]{1,0:T(8,128)S(1)}, f32[48,128]{1,0:T(8,128)S(1)}, u32[]{:S(2)}, u32[]{:S(2)}) %collective-permute-start) | collective-permute-done | bytes 24608 | tf_op jit(solution)/shard_map/ppermute | solution.py:256
  8.2 0.0 copy-done.2
  8.2 18.8 %all-gather.2.parts_ref = f32[4,51,128]{2,1,0:T(8,128)S(1)} all-gather(f32[1,51,128]{2,1,0:T(8,128)S(1)} %bitcast.5), channel_id=2, replica_groups={{0,8,16,24},{2,10,18,26},{4,12,20,28},{6,14,22,30},{1,9,17,25},{3,11,19..., dimensions={0}, use_global_device_ids=true | all-gather | bytes 130560 | tf_op jit(solution)/shard_map/all_gather | solution.py:325
  27.1 6.9 %all-gather.3.parts_ref = f32[4,60,128]{2,1,0:T(8,128)S(1)} all-gather(f32[1,60,128]{2,1,0:T(8,128)S(1)} %bitcast.4), channel_id=3, replica_groups={{0,2,4,6},{8,10,12,14},{16,18,20,22},{24,26,28,30},{1,3,5,7},{9,11,13,1..., dimensions={0}, use_global_device_ids=true | all-gather | bytes 153600 | tf_op jit(solution)/shard_map/all_gather | solution.py:325
  34.0 0.0 copy-start
  34.0 0.0 copy-start.1
  34.1 0.1 collective-permute-start.1
  34.1 1.2 %collective-permute-done.1.arrived_ref = f32[48,128]{1,0:T(8,128)S(1)} collective-permute-done((f32[48,128]{1,0:T(8,128)S(1)}, f32[48,128]{1,0:T(8,128)S(1)}, u32[]{:S(2)}, u32[]{:S(2)}) %collective-permute-start.1) | collective-permute-done | bytes 24608 | tf_op jit(solution)/shard_map/ppermute | solution.py:256
  35.3 0.0 copy-done
  35.3 0.0 copy-done.1
  35.3 0.9 %sphere_velocities.1 = (f32[6,128]{1,0:T(8,128)}, f32[3,4096]{1,0:T(4,128)}) custom-call(f32[48,128]{1,0:T(8,128)S(1)} %clump_update.1.mine_ref, f32[48,128]{1,0:T(8,128)S(1)} %collective-permute-done.1.arrived_ref, f32[3,4096]{1,0:T(4,128)S(1)} %copy-done, s32[1,4096]{1,0:T(1,128)S(1)} %bitcast.7), custom_call_target="tpu_custom_call" | custom-call | tf_op jit(solution)/shard_map/sphere_velocities/pallas_call | solution.py:335
  (3 shorter events, 0.0 us)
Async XLA Ops:
  6.9 1.3 %copy-start.2 = (f32[4,128]{1,0:T(4,128)S(1)}, f32[4,128]{1,0:T(4,128)}, u32[]{:S(2)}) copy-start(f32[4,128]{1,0:T(4,128)} %inverse_ref.1) | copy-start | bytes 6148
  7.0 1.3 %collective-permute-start = (f32[48,128]{1,0:T(8,128)S(1)}, f32[48,128]{1,0:T(8,128)S(1)}, u32[]{:S(2)}, u32[]{:S(2)}) collective-permute-start(f32[48,128]{1,0:T(8,128)S(1)} %get-tuple-element.5), channel_id=1, source_target_pairs={{0,1},{1,0},{2,3},{3,2},{4,5},{5,4},{6,7},{7,6},{8,9},{9,8},{10,11... | collective-permute-start | bytes 73736 | tf_op jit(solution)/shard_map/ppermute | solution.py:256
  34.0 1.3 %copy-start = (f32[3,4096]{1,0:T(4,128)S(1)}, f32[3,4096]{1,0:T(4,128)}, u32[]{:S(2)}) copy-start(f32[3,4096]{1,0:T(4,128)} %offset_ref.1) | copy-start | bytes 147460
  34.0 1.3 %copy-start.1 = (s32[4096]{0:T(1024)S(1)}, s32[4096]{0:T(1024)}, u32[]{:S(2)}) copy-start(s32[4096]{0:T(1024)} %param.13) | copy-start | bytes 49156
  34.1 1.3 %collective-permute-start.1 = (f32[48,128]{1,0:T(8,128)S(1)}, f32[48,128]{1,0:T(8,128)S(1)}, u32[]{:S(2)}, u32[]{:S(2)}) collective-permute-start(f32[48,128]{1,0:T(8,128)S(1)} %clump_update.1.mine_ref), channel_id=1, source_target_pairs={{0,1},{1,0},{2,3},{3,2},{4,5},{5,4},{6,7},{7,6},{8,9},{9,8},{10,11... | collective-permute-start | bytes 73736 | tf_op jit(solution)/shard_map/ppermute | solution.py:256

commit v5 on v1

--- a/solution.py
+++ b/solution.py
@@ -10,7 +10,7 @@
 
 TILE = 128
 SLOT = 256
-UNROLL = 8
+UNROLL = 4
 LANES = 16
 BLOCK = TILE // LANES
 
@@ -213,11 +213,13 @@
 
 def update_kernel(partners, *refs):
     *parts, out_ref, inverse_ref = refs
-    owners = len(partners)
+    owners = len(partners[0])
     rows = 3 * owners
     held = owners // len(parts)
     me = lax.axis_index("space")
-    for k, partner in enumerate(partners):
+    first_core = lax.axis_index("sub") == 0
+    for k in range(owners):
+        partner = jnp.where(first_core, partners[0][k], partners[1][k])
         first = rows + 3 * (k % held)
         inverse_ref[me ^ partner] = parts[k // held][first : first + 3, :]
     out_ref[...] = sum_rows(parts, rows) * jnp.concatenate([inverse_ref[k] for k in range(owners)], axis=0)
@@ -255,9 +257,28 @@
     clump_ref[...] = velocity_ref[lax.axis_index("space")]
 
 
-def swap(value, axis, bit):
-    size = lax.axis_size(axis)
-    return lax.ppermute(value, axis, [(k, k ^ bit) for k in range(size)])
+def swap_cores(value):
+    return lax.ppermute(value, "sub", [(0, 1), (1, 0)])
+
+
+def swap(value, bits):
+    chips = range(lax.axis_size("space"))
+    pairs = [(2 * k + core, 2 * (k ^ bit) + core) for k in chips for core, bit in enumerate(bits)]
+    return lax.ppermute(value, ("space", "sub"), pairs)
+
+
+def steps_of(owners):
+    pairs, left = [], owners
+    while left > 2:
+        pairs.append((left // 2, left // 4))
+        left //= 4
+    rest = [(1,)] * (left == 2)
+    return pairs[1:] + pairs[:1] + rest, pairs + rest
+
+
+def partners_of(steps):
+    bits = [bit for step in steps for bit in step]
+    return [sum(bit for n, bit in enumerate(bits) if k >> n & 1) for k in range(2 ** len(bits))]
 
 
 def per_device(
@@ -315,19 +336,15 @@
             name=name,
         )(*operands)
 
-    mine = small(first_kernel, rows + 3, "core_sum", keep, swap(send, "sub", 1), clump_inverse)
-    bits = []
-    left = owners
-    while left > 1:
-        step = [left // 2, left // 4] if left > 2 else [1]
-        left //= 2 ** len(step)
-        bits += step
-        others = step if len(step) == 1 else [*step, sum(step)]
-        parts = [mine] + [swap(mine, "space", bit) for bit in others]
-        if left > 1:
+    mine = small(first_kernel, rows + 3, "core_sum", keep, swap_cores(send), clump_inverse)
+    steps = steps_of(owners)
+    for number, step in enumerate(zip(*steps)):
+        both = [[*bits, sum(bits)] if len(bits) == 2 else bits for bits in step]
+        parts = [mine] + [swap(mine, bits) for bits in zip(*both)]
+        if number < len(steps[0]) - 1:
             height = rows + len(parts) * (mine.shape[0] - rows)
             mine = small(functools.partial(join_kernel, rows), height, "space_sum", *parts)
-    partners = [sum(bit for n, bit in enumerate(bits) if k >> n & 1) for k in range(owners)]
+    partners = [partners_of(core_steps) for core_steps in steps]
     velocities = small(
         functools.partial(update_kernel, partners), rows, "clump_update", *parts,
         scratch=[pltpu.VMEM((owners, 3, clumps), f32)],
@@ -344,7 +361,7 @@
         scratch_shapes=[pltpu.VMEM((owners, 6, clumps), f32)],
         compiler_params=params,
         name="sphere_velocities",
-    )(velocities, swap(velocities, "sub", 1), sphere_offset, ids)
+    )(velocities, swap_cores(velocities), sphere_offset, ids)
 
 
 def solution(mesh):

time: 29.1 us -> 29 us (level)
  Pallas kernels: 6.62 us -> 9.54 us
  waiting for transfers between devices: 10.3 us -> 7.48 us
    pallas_call x1, Pallas kernels: 5.66 us -> 8.58 us  [per_device(): pl.pallas_call(loads_kernel, out_shape=(pltpu.VMEM((rows, clumps), f32),...]
    ppermute x8, waiting for transfers between devices: 10.3 us -> 7.48 us  [the longest x6 5.12 us: swap(): return lax.ppermute(value, ('space', 'sub'), pairs)]
  transfers between devices with their start and end apart: 8 -> 8, of which waited for: 8 -> 6; matrix products, arithmetic and copies ran while one was open for 0% -> 0% of each run, Pallas kernels for 0% -> 0%
where the time goes in v5:
time: 29 us; the launch traced here: 29.1 us
  starting transfers between devices  10.7 us (37%)
  Pallas kernels  9.54 us (33%)
  waiting for transfers between devices  7.48 us (26%)
  between operations  1.35 us (5%)
    ppermute x6, starting transfers between devices, swap(): return lax.ppermute(value, ('space', 'sub'), pairs)  10.5 us
    pallas_call x1, Pallas kernels, per_device(): pl.pallas_call(loads_kernel, out_shape=(pltpu.VMEM((rows, clumps), f32),...  8.58 us
    ppermute x6, waiting for transfers between devices, swap(): return lax.ppermute(value, ('space', 'sub'), pairs)  5.12 us
    ppermute x2, waiting for transfers between devices, swap_cores(): return lax.ppermute(value, 'sub', [(0, 1), (1, 0)])  2.36 us
    pallas_call x1, Pallas kernels, per_device(): pl.pallas_call(velocity_kernel, out_shape=(jax.ShapeDtypeStruct((6, clump...  0.91 us
  transfers between devices with their start and end apart: 8, of which 6 were waited for; matrix products, arithmetic and copies ran while one was open for 0% of the time, Pallas kernels for 0%

profile of v5, /device:TPU:0, one launch (start us, length us, event | category | flops | bytes accessed | tf_op | source)
XLA Modules:
  0.0 29.1 jit_solution(8800927352282454162)
XLA Ops:
  1.3 8.6 %clump_loads.1 = (f32[48,128]{1,0:T(8,128)S(1)}, f32[48,128]{1,0:T(8,128)S(1)}) custom-call(s32[1]{0:T(128)S(6)} %copy.10.count_ref, s32[2,128]{1,0:T(2,128)} %bitcast.4, f32[8,4096]{1,0:T(8,128)} %fluid_hbm.1, f32[7,4096]{1,0:T(8,128)} %sphere_hbm.1, f32[3,4096]{1,0:T(4,128)} %offset_ref.1, s32[1,4096]{1,0:T(1,128)} %bitcast.2, f32[6,128]{1,0:T(8,128)} %state_hbm.1, ...), custom_call_target="tpu_custom_call" | custom-call | tf_op jit(solution)/shard_map/clump_loads/pallas_call | solution.py:298
  9.9 0.0 copy-start.2
  9.9 0.1 collective-permute-start
  10.0 1.2 %collective-permute-done.arrived_ref = f32[48,128]{1,0:T(8,128)S(1)} collective-permute-done((f32[48,128]{1,0:T(8,128)S(1)}, f32[48,128]{1,0:T(8,128)S(1)}, u32[]{:S(2)}, u32[]{:S(2)}) %collective-permute-start) | collective-permute-done | bytes 24608 | tf_op jit(solution)/shard_map/ppermute | solution.py:261
  11.1 0.0 copy-done.2
  11.2 5.5 %collective-permute-start.3 = (f32[51,128]{1,0:T(8,128)S(1)}, f32[51,128]{1,0:T(8,128)S(1)}, u32[]{:S(2)}, u32[]{:S(2)}) collective-permute-start(f32[51,128]{1,0:T(8,128)S(1)} %core_sum.1.refs_0_), channel_id=1, source_target_pairs={{0,6},{1,25},{2,4},{3,27},{4,2},{5,29},{6,0},{7,31},{8,14},{9,17},... | collective-permute-start | bytes 78344 | tf_op jit(solution)/shard_map/ppermute | solution.py:267
  16.6 0.0 collective-permute-start.2
  16.6 0.6 %collective-permute-start.1 = (f32[51,128]{1,0:T(8,128)S(1)}, f32[51,128]{1,0:T(8,128)S(1)}, u32[]{:S(2)}, u32[]{:S(2)}) collective-permute-start(f32[51,128]{1,0:T(8,128)S(1)} %core_sum.1.refs_0_), channel_id=1, source_target_pairs={{0,4},{1,17},{2,6},{3,19},{4,0},{5,21},{6,2},{7,23},{8,12},{9,25},... | collective-permute-start | bytes 78344 | tf_op jit(solution)/shard_map/ppermute | solution.py:267
  17.2 1.2 %collective-permute-done.3.refs_3_ = f32[51,128]{1,0:T(8,128)S(1)} collective-permute-done((f32[51,128]{1,0:T(8,128)S(1)}, f32[51,128]{1,0:T(8,128)S(1)}, u32[]{:S(2)}, u32[]{:S(2)}) %collective-permute-start.3) | collective-permute-done | bytes 26144 | tf_op jit(solution)/shard_map/ppermute | solution.py:267
  18.5 2.0 %collective-permute-done.2.refs_2_ = f32[51,128]{1,0:T(8,128)S(1)} collective-permute-done((f32[51,128]{1,0:T(8,128)S(1)}, f32[51,128]{1,0:T(8,128)S(1)}, u32[]{:S(2)}, u32[]{:S(2)}) %collective-permute-start.2) | collective-permute-done | bytes 26144 | tf_op jit(solution)/shard_map/ppermute | solution.py:267
  20.5 0.0 collective-permute-done.1.refs_1_
  20.5 0.0 copy-start
  20.5 0.0 copy-start.1
  20.5 1.0 %collective-permute-start.6 = (f32[60,128]{1,0:T(8,128)S(1)}, f32[60,128]{1,0:T(8,128)S(1)}, u32[]{:S(2)}, u32[]{:S(2)}) collective-permute-start(f32[60,128]{1,0:T(8,128)S(1)} %space_sum.1.refs_0_), channel_id=1, source_target_pairs={{0,24},{1,7},{2,26},{3,5},{4,28},{5,3},{6,30},{7,1},{8,16},{9,15},... | collective-permute-start | bytes 92168 | tf_op jit(solution)/shard_map/ppermute | solution.py:267
  21.5 0.0 collective-permute-start.5
  21.5 3.5 %collective-permute-start.4 = (f32[60,128]{1,0:T(8,128)S(1)}, f32[60,128]{1,0:T(8,128)S(1)}, u32[]{:S(2)}, u32[]{:S(2)}) collective-permute-start(f32[60,128]{1,0:T(8,128)S(1)} %space_sum.1.refs_0_), channel_id=1, source_target_pairs={{0,16},{1,5},{2,18},{3,7},{4,20},{5,1},{6,22},{7,3},{8,24},{9,13},... | collective-permute-start | bytes 92168 | tf_op jit(solution)/shard_map/ppermute | solution.py:267
  25.0 1.3 %collective-permute-done.6.refs_3_ = f32[60,128]{1,0:T(8,128)S(1)} collective-permute-done((f32[60,128]{1,0:T(8,128)S(1)}, f32[60,128]{1,0:T(8,128)S(1)}, u32[]{:S(2)}, u32[]{:S(2)}) %collective-permute-start.6) | collective-permute-done | bytes 30752 | tf_op jit(solution)/shard_map/ppermute | solution.py:267
  26.3 0.0 collective-permute-done.5.refs_2_
  26.3 0.6 %collective-permute-done.4.refs_1_ = f32[60,128]{1,0:T(8,128)S(1)} collective-permute-done((f32[60,128]{1,0:T(8,128)S(1)}, f32[60,128]{1,0:T(8,128)S(1)}, u32[]{:S(2)}, u32[]{:S(2)}) %collective-permute-start.4) | collective-permute-done | bytes 30752 | tf_op jit(solution)/shard_map/ppermute | solution.py:267
  26.9 0.1 collective-permute-start.7
  27.0 1.2 %collective-permute-done.7.arrived_ref = f32[48,128]{1,0:T(8,128)S(1)} collective-permute-done((f32[48,128]{1,0:T(8,128)S(1)}, f32[48,128]{1,0:T(8,128)S(1)}, u32[]{:S(2)}, u32[]{:S(2)}) %collective-permute-start.7) | collective-permute-done | bytes 24608 | tf_op jit(solution)/shard_map/ppermute | solution.py:261
  28.2 0.0 copy-done
  28.2 0.0 copy-done.1
  28.2 0.9 %sphere_velocities.1 = (f32[6,128]{1,0:T(8,128)}, f32[3,4096]{1,0:T(4,128)}) custom-call(f32[48,128]{1,0:T(8,128)S(1)} %clump_update.1.mine_ref, f32[48,128]{1,0:T(8,128)S(1)} %collective-permute-done.7.arrived_ref, f32[3,4096]{1,0:T(4,128)S(1)} %copy-done, s32[1,4096]{1,0:T(1,128)S(1)} %bitcast.3), custom_call_target="tpu_custom_call" | custom-call | tf_op jit(solution)/shard_map/sphere_velocities/pallas_call | solution.py:353
  (3 shorter events, 0.1 us)
Async XLA Ops:
  9.9 1.3 %copy-start.2 = (f32[4,128]{1,0:T(4,128)S(1)}, f32[4,128]{1,0:T(4,128)}, u32[]{:S(2)}) copy-start(f32[4,128]{1,0:T(4,128)} %inverse_ref.1) | copy-start | bytes 6148
  9.9 1.3 %collective-permute-start = (f32[48,128]{1,0:T(8,128)S(1)}, f32[48,128]{1,0:T(8,128)S(1)}, u32[]{:S(2)}, u32[]{:S(2)}) collective-permute-start(f32[48,128]{1,0:T(8,128)S(1)} %get-tuple-element.5), channel_id=1, source_target_pairs={{0,1},{1,0},{2,3},{3,2},{4,5},{5,4},{6,7},{7,6},{8,9},{9,8},{10,11... | collective-permute-start | bytes 73736 | tf_op jit(solution)/shard_map/ppermute | solution.py:261
  11.2 7.3 %collective-permute-start.3 = (f32[51,128]{1,0:T(8,128)S(1)}, f32[51,128]{1,0:T(8,128)S(1)}, u32[]{:S(2)}, u32[]{:S(2)}) collective-permute-start(f32[51,128]{1,0:T(8,128)S(1)} %core_sum.1.refs_0_), channel_id=1, source_target_pairs={{0,6},{1,25},{2,4},{3,27},{4,2},{5,29},{6,0},{7,31},{8,14},{9,17},... | collective-permute-start | bytes 78344 | tf_op jit(solution)/shard_map/ppermute | solution.py:267
  16.6 3.9 %collective-permute-start.2 = (f32[51,128]{1,0:T(8,128)S(1)}, f32[51,128]{1,0:T(8,128)S(1)}, u32[]{:S(2)}, u32[]{:S(2)}) collective-permute-start(f32[51,128]{1,0:T(8,128)S(1)} %core_sum.1.refs_0_), channel_id=1, source_target_pairs={{0,2},{1,9},{2,0},{3,11},{4,6},{5,13},{6,4},{7,15},{8,10},{9,1},{1... | collective-permute-start | bytes 78344 | tf_op jit(solution)/shard_map/ppermute | solution.py:267
  16.6 3.9 %collective-permute-start.1 = (f32[51,128]{1,0:T(8,128)S(1)}, f32[51,128]{1,0:T(8,128)S(1)}, u32[]{:S(2)}, u32[]{:S(2)}) collective-permute-start(f32[51,128]{1,0:T(8,128)S(1)} %core_sum.1.refs_0_), channel_id=1, source_target_pairs={{0,4},{1,17},{2,6},{3,19},{4,0},{5,21},{6,2},{7,23},{8,12},{9,25},... | collective-permute-start | bytes 78344 | tf_op jit(solution)/shard_map/ppermute | solution.py:267
  20.5 7.7 %copy-start = (f32[3,4096]{1,0:T(4,128)S(1)}, f32[3,4096]{1,0:T(4,128)}, u32[]{:S(2)}) copy-start(f32[3,4096]{1,0:T(4,128)} %offset_ref.1) | copy-start | bytes 147460
  20.5 7.7 %copy-start.1 = (s32[4096]{0:T(1024)S(1)}, s32[4096]{0:T(1024)}, u32[]{:S(2)}) copy-start(s32[4096]{0:T(1024)} %param.13) | copy-start | bytes 49156
  20.5 5.8 %collective-permute-start.6 = (f32[60,128]{1,0:T(8,128)S(1)}, f32[60,128]{1,0:T(8,128)S(1)}, u32[]{:S(2)}, u32[]{:S(2)}) collective-permute-start(f32[60,128]{1,0:T(8,128)S(1)} %space_sum.1.refs_0_), channel_id=1, source_target_pairs={{0,24},{1,7},{2,26},{3,5},{4,28},{5,3},{6,30},{7,1},{8,16},{9,15},... | collective-permute-start | bytes 92168 | tf_op jit(solution)/shard_map/ppermute | solution.py:267
  21.5 4.8 %collective-permute-start.5 = (f32[60,128]{1,0:T(8,128)S(1)}, f32[60,128]{1,0:T(8,128)S(1)}, u32[]{:S(2)}, u32[]{:S(2)}) collective-permute-start(f32[60,128]{1,0:T(8,128)S(1)} %space_sum.1.refs_0_), channel_id=1, source_target_pairs={{0,8},{1,3},{2,10},{3,1},{4,12},{5,7},{6,14},{7,5},{8,0},{9,11},{1... | collective-permute-start | bytes 92168 | tf_op jit(solution)/shard_map/ppermute | solution.py:267
  21.5 5.4 %collective-permute-start.4 = (f32[60,128]{1,0:T(8,128)S(1)}, f32[60,128]{1,0:T(8,128)S(1)}, u32[]{:S(2)}, u32[]{:S(2)}) collective-permute-start(f32[60,128]{1,0:T(8,128)S(1)} %space_sum.1.refs_0_), channel_id=1, source_target_pairs={{0,16},{1,5},{2,18},{3,7},{4,20},{5,1},{6,22},{7,3},{8,24},{9,13},... | collective-permute-start | bytes 92168 | tf_op jit(solution)/shard_map/ppermute | solution.py:267
  26.9 1.3 %collective-permute-start.7 = (f32[48,128]{1,0:T(8,128)S(1)}, f32[48,128]{1,0:T(8,128)S(1)}, u32[]{:S(2)}, u32[]{:S(2)}) collective-permute-start(f32[48,128]{1,0:T(8,128)S(1)} %clump_update.1.mine_ref), channel_id=1, source_target_pairs={{0,1},{1,0},{2,3},{3,2},{4,5},{5,4},{6,7},{7,6},{8,9},{9,8},{10,11... | collective-permute-start | bytes 73736 | tf_op jit(solution)/shard_map/ppermute | solution.py:261

commit v6 on v1

--- a/solution.py
+++ b/solution.py
@@ -74,6 +74,7 @@
         copy.start()
 
     acc_ref[...] = jnp.zeros_like(acc_ref)
+    weight_ref[...] = jnp.zeros_like(weight_ref)
 
     lane = lax.broadcasted_iota(jnp.int32, (TILE, 3 * TILE), 0)
     target = lax.broadcasted_iota(jnp.int32, (TILE, 3 * TILE), 1) // TILE
@@ -106,7 +107,7 @@
     place_ref[...] = sphere_ref[0:3, :] * (1.0 / support_radius) - 1.0
     copies[2].wait()
 
-    def pair_weights(slot, part):
+    def pair_weights(slot):
         a = list_ref[0, slot]
         b = list_ref[1, slot]
         cols = pl.ds(pl.multiple_of(a * TILE, TILE), TILE)
@@ -116,34 +117,29 @@
         square = jnp.maximum(dx * dx + dy * dy + dz * dz, 1e-30)
         falloff = jnp.maximum(1.0 - square * lax.rsqrt(square), 0.0)
         high, low = split_two(falloff * falloff * falloff)
-        weight_ref[part, 0:TILE, :] = high
-        weight_ref[part, TILE:, :] = low
-
-    def add_sums(slot, part, live):
-        a = list_ref[0, slot]
-        b = list_ref[1, slot]
-        cols = pl.ds(pl.multiple_of(a * TILE, TILE), TILE)
-        sums = jnp.dot(terms_ref[b], weight_ref[part], preferred_element_type=f32)
+        return jnp.concatenate([high, low], axis=0)
+
+    count = count_ref[0]
+    last = list_ref.shape[1] - 1
+
+    def add_sums(slot, weights):
+        here = jnp.clip(slot, 0, last)
+        live = jnp.where((slot >= 0) & (slot < count), 1.0, 0.0).astype(f32)
+        cols = pl.ds(pl.multiple_of(list_ref[0, here] * TILE, TILE), TILE)
+        sums = jnp.dot(terms_ref[list_ref[1, here]], weights, preferred_element_type=f32)
         acc_ref[:, cols] += live * (sums[0:16] + sums[16:32])
 
-    count = count_ref[0]
-    trips = (count + UNROLL - 1) // UNROLL
-    last = list_ref.shape[1] - 1
-
-    for part in range(UNROLL):
-        pair_weights(min(part, last), part)
-
-    @pl.loop(1, trips)
-    def _(trip):
-        for part in range(UNROLL):
-            add_sums((trip - 1) * UNROLL + part, part, 1.0)
-        for part in range(UNROLL):
-            pair_weights(jnp.minimum(trip * UNROLL + part, last), part)
-
-    for part in range(UNROLL):
-        slot = (trips - 1) * UNROLL + part
-        live = jnp.where(slot < count, 1.0, 0.0).astype(f32)
-        add_sums(jnp.clip(slot, 0, last), part, live)
+    groups = (count + UNROLL - 1) // UNROLL
+
+    @pl.loop(0, groups)
+    def _(number):
+        first = number * UNROLL
+        add_sums(first - 1, weight_ref[...])
+        for part in range(UNROLL - 1):
+            add_sums(first + part, pair_weights(jnp.minimum(first + part, last)))
+        weight_ref[...] = pair_weights(jnp.minimum(first + UNROLL - 1, last))
+
+    add_sums(groups * UNROLL - 1, weight_ref[...])
 
     for copy in copies[3:]:
         copy.wait()
@@ -223,13 +219,18 @@
     out_ref[...] = sum_rows(parts, rows) * jnp.concatenate([inverse_ref[k] for k in range(owners)], axis=0)
 
 
-def velocity_kernel(mine_ref, arrived_ref, offset_ref, ids_ref, clump_ref, sphere_ref, velocity_ref):
+def velocity_kernel(
+    mine_ref, arrived_ref, offset_ref, ids_ref, clump_ref, sphere_hbm, velocity_ref, sphere_ref, sent
+):
     owners, _, clumps = velocity_ref.shape
     group = group_of(owners)
     core = lax.axis_index("sub")
 
+    part = math.gcd(group, 4)
+
     @pl.loop(0, owners // group)
     def _(block):
+        copies = []
         rows = pl.ds(pl.multiple_of(block * (3 * group), math.gcd(3 * group, 8)), 3 * group)
         mine = mine_ref[rows, :]
         arrived = arrived_ref[rows, :]
@@ -251,6 +252,15 @@
             offset = offset_ref[:, here]
             turn = cross([picked[3 + i : 4 + i] for i in range(3)], [offset[i : i + 1] for i in range(3)])
             sphere_ref[:, here] = picked[0:3] + jnp.concatenate(turn, axis=0)
+            if (k + 1) % part == 0:
+                start = pl.multiple_of((owner + 1 - part) * SLOT, SLOT)
+                done = pl.ds(start, part * SLOT)
+                copies.append(
+                    pltpu.make_async_copy(sphere_ref.at[:, done], sphere_hbm.at[:, done], sent.at[k // part])
+                )
+                copies[-1].start()
+        for copy in copies:
+            copy.wait()
 
     clump_ref[...] = velocity_ref[lax.axis_index("space")]
 
@@ -292,7 +302,7 @@
             pltpu.VMEM((BLOCK, TILE, 3 * TILE), bf16),
             pltpu.VMEM((fluid // TILE, TILE, 3 * TILE), f32),
             pltpu.VMEM((fluid // TILE, 32, 2 * TILE), bf16),
-            pltpu.VMEM((UNROLL, 2 * TILE, TILE), bf16),
+            pltpu.VMEM((2 * TILE, TILE), bf16),
             pltpu.VMEM((16, spheres), f32),
         ],
         compiler_params=params,
@@ -340,8 +350,12 @@
             jax.ShapeDtypeStruct((3, spheres), f32),
         ),
         in_specs=[vmem] * 4,
-        out_specs=(vmem, vmem),
-        scratch_shapes=[pltpu.VMEM((owners, 6, clumps), f32)],
+        out_specs=(vmem, hbm),
+        scratch_shapes=[
+            pltpu.VMEM((owners, 6, clumps), f32),
+            pltpu.VMEM((3, spheres), f32),
+            pltpu.SemaphoreType.DMA((group_of(owners),)),
+        ],
         compiler_params=params,
         name="sphere_velocities",
     )(velocities, swap(velocities, "sub", 1), sphere_offset, ids)

time: 29.1 us -> 32 us (1.100); the launches traced: 29 us -> 32.5 us
  Pallas kernels: 6.62 us -> 8.65 us
  starting transfers between devices: 10.7 us -> 11.5 us
  waiting for transfers between devices: 10.3 us -> 11 us
    pallas_call x1, Pallas kernels: 5.66 us -> 6.99 us  [per_device(): pl.pallas_call(loads_kernel, out_shape=(pltpu.VMEM((rows, clumps), f32),...]
    ppermute x8, starting transfers between devices: 10.7 us -> 11.5 us  [swap(): return lax.ppermute(value, axis, [(k, k ^ bit) for k in range(size)])]
    ppermute x8, waiting for transfers between devices: 10.3 us -> 11 us  [swap(): return lax.ppermute(value, axis, [(k, k ^ bit) for k in range(size)])]
    pallas_call x1, Pallas kernels: 0.91 us -> 1.62 us  [per_device(): pl.pallas_call(velocity_kernel, out_shape=(jax.ShapeDtypeStruct((6, clump...]
  transfers between devices with their start and end apart: 8 -> 8, of which waited for: 8 -> 7; matrix products, arithmetic and copies ran while one was open for 0% -> 0% of each run, Pallas kernels for 0% -> 0%
where the time goes in v6:
time: 32 us; the launch traced here: 32.5 us
  starting transfers between devices  11.5 us (36%)
  waiting for transfers between devices  11 us (34%)
  Pallas kernels  8.65 us (27%)
  between operations  1.35 us (4%)
    ppermute x8, starting transfers between devices, swap(): return lax.ppermute(value, axis, [(k, k ^ bit) for k in range(size)])  11.5 us
    ppermute x8, waiting for transfers between devices, swap(): return lax.ppermute(value, axis, [(k, k ^ bit) for k in range(size)])  11 us
    pallas_call x1, Pallas kernels, per_device(): pl.pallas_call(loads_kernel, out_shape=(pltpu.VMEM((rows, clumps), f32),...  6.99 us
    pallas_call x1, Pallas kernels, per_device(): pl.pallas_call(velocity_kernel, out_shape=(jax.ShapeDtypeStruct((6, clump...  1.62 us
  transfers between devices with their start and end apart: 8, of which 7 were waited for; matrix products, arithmetic and copies ran while one was open for 0% of the time, Pallas kernels for 0%

profile of v6, /device:TPU:0, one launch (start us, length us, event | category | flops | bytes accessed | tf_op | source)
XLA Modules:
  0.0 32.5 jit_solution(13830692654407408773)
XLA Ops:
  1.3 7.0 %clump_loads.1 = (f32[48,128]{1,0:T(8,128)S(1)}, f32[48,128]{1,0:T(8,128)S(1)}) custom-call(s32[1]{0:T(128)S(6)} %copy.10.count_ref, s32[2,128]{1,0:T(2,128)} %bitcast.4, f32[8,4096]{1,0:T(8,128)} %fluid_hbm.1, f32[7,4096]{1,0:T(8,128)} %sphere_hbm.1, f32[3,4096]{1,0:T(4,128)} %offset_ref.1, s32[1,4096]{1,0:T(1,128)} %bitcast.2, f32[6,128]{1,0:T(8,128)} %state_hbm.1, ...), custom_call_target="tpu_custom_call" | custom-call | tf_op jit(solution)/shard_map/clump_loads/pallas_call | solution.py:287
  8.3 0.0 copy-start.2
  8.3 0.1 collective-permute-start
  8.4 1.2 %collective-permute-done.arrived_ref = f32[48,128]{1,0:T(8,128)S(1)} collective-permute-done((f32[48,128]{1,0:T(8,128)S(1)}, f32[48,128]{1,0:T(8,128)S(1)}, u32[]{:S(2)}, u32[]{:S(2)}) %collective-permute-start) | collective-permute-done | bytes 24608 | tf_op jit(solution)/shard_map/ppermute | solution.py:270
  9.5 0.0 copy-done.2
  9.6 4.2 %collective-permute-start.3 = (f32[51,128]{1,0:T(8,128)S(1)}, f32[51,128]{1,0:T(8,128)S(1)}, u32[]{:S(2)}, u32[]{:S(2)}) collective-permute-start(f32[51,128]{1,0:T(8,128)S(1)} %core_sum.1.refs_0_), channel_id=1, source_target_pairs={{0,24},{2,26},{4,28},{6,30},{8,16},{10,18},{12,20},{14,22},{16,8},... | collective-permute-start | bytes 78344 | tf_op jit(solution)/shard_map/ppermute | solution.py:270
  13.8 0.9 %collective-permute-start.2 = (f32[51,128]{1,0:T(8,128)S(1)}, f32[51,128]{1,0:T(8,128)S(1)}, u32[]{:S(2)}, u32[]{:S(2)}) collective-permute-start(f32[51,128]{1,0:T(8,128)S(1)} %core_sum.1.refs_0_), channel_id=1, source_target_pairs={{0,8},{2,10},{4,12},{6,14},{8,0},{10,2},{12,4},{14,6},{16,24},{18,... | collective-permute-start | bytes 78344 | tf_op jit(solution)/shard_map/ppermute | solution.py:270
  14.7 0.0 collective-permute-start.1
  14.7 1.1 %collective-permute-done.3.refs_3_ = f32[51,128]{1,0:T(8,128)S(1)} collective-permute-done((f32[51,128]{1,0:T(8,128)S(1)}, f32[51,128]{1,0:T(8,128)S(1)}, u32[]{:S(2)}, u32[]{:S(2)}) %collective-permute-start.3) | collective-permute-done | bytes 26144 | tf_op jit(solution)/shard_map/ppermute | solution.py:270
  15.8 1.9 %collective-permute-done.2.refs_2_ = f32[51,128]{1,0:T(8,128)S(1)} collective-permute-done((f32[51,128]{1,0:T(8,128)S(1)}, f32[51,128]{1,0:T(8,128)S(1)}, u32[]{:S(2)}, u32[]{:S(2)}) %collective-permute-start.2) | collective-permute-done | bytes 26144 | tf_op jit(solution)/shard_map/ppermute | solution.py:270
  17.7 1.8 %collective-permute-done.1.refs_1_ = f32[51,128]{1,0:T(8,128)S(1)} collective-permute-done((f32[51,128]{1,0:T(8,128)S(1)}, f32[51,128]{1,0:T(8,128)S(1)}, u32[]{:S(2)}, u32[]{:S(2)}) %collective-permute-start.1) | collective-permute-done | bytes 26144 | tf_op jit(solution)/shard_map/ppermute | solution.py:270
  19.5 0.0 copy-start
  19.5 0.0 copy-start.1
  19.5 2.1 %collective-permute-start.6 = (f32[60,128]{1,0:T(8,128)S(1)}, f32[60,128]{1,0:T(8,128)S(1)}, u32[]{:S(2)}, u32[]{:S(2)}) collective-permute-start(f32[60,128]{1,0:T(8,128)S(1)} %space_sum.1.refs_0_), channel_id=1, source_target_pairs={{0,6},{2,4},{4,2},{6,0},{8,14},{10,12},{12,10},{14,8},{16,22},{18,... | collective-permute-start | bytes 92168 | tf_op jit(solution)/shard_map/ppermute | solution.py:270
  21.6 4.1 %collective-permute-start.5 = (f32[60,128]{1,0:T(8,128)S(1)}, f32[60,128]{1,0:T(8,128)S(1)}, u32[]{:S(2)}, u32[]{:S(2)}) collective-permute-start(f32[60,128]{1,0:T(8,128)S(1)} %space_sum.1.refs_0_), channel_id=1, source_target_pairs={{0,2},{2,0},{4,6},{6,4},{8,10},{10,8},{12,14},{14,12},{16,18},{18,... | collective-permute-start | bytes 92168 | tf_op jit(solution)/shard_map/ppermute | solution.py:270
  25.7 0.0 collective-permute-start.4
  25.7 0.0 collective-permute-done.6.refs_3_
  25.7 2.2 %collective-permute-done.5.refs_2_ = f32[60,128]{1,0:T(8,128)S(1)} collective-permute-done((f32[60,128]{1,0:T(8,128)S(1)}, f32[60,128]{1,0:T(8,128)S(1)}, u32[]{:S(2)}, u32[]{:S(2)}) %collective-permute-start.5) | collective-permute-done | bytes 30752 | tf_op jit(solution)/shard_map/ppermute | solution.py:270
  27.9 1.7 %collective-permute-done.4.refs_1_ = f32[60,128]{1,0:T(8,128)S(1)} collective-permute-done((f32[60,128]{1,0:T(8,128)S(1)}, f32[60,128]{1,0:T(8,128)S(1)}, u32[]{:S(2)}, u32[]{:S(2)}) %collective-permute-start.4) | collective-permute-done | bytes 30752 | tf_op jit(solution)/shard_map/ppermute | solution.py:270
  29.6 0.1 collective-permute-start.7
  29.7 1.2 %collective-permute-done.7.arrived_ref = f32[48,128]{1,0:T(8,128)S(1)} collective-permute-done((f32[48,128]{1,0:T(8,128)S(1)}, f32[48,128]{1,0:T(8,128)S(1)}, u32[]{:S(2)}, u32[]{:S(2)}) %collective-permute-start.7) | collective-permute-done | bytes 24608 | tf_op jit(solution)/shard_map/ppermute | solution.py:270
  30.9 0.0 copy-done
  30.9 0.0 copy-done.1
  30.9 1.6 %sphere_velocities.1 = (f32[6,128]{1,0:T(8,128)}, f32[3,4096]{1,0:T(4,128)}) custom-call(f32[48,128]{1,0:T(8,128)S(1)} %clump_update.1.mine_ref, f32[48,128]{1,0:T(8,128)S(1)} %collective-permute-done.7.arrived_ref, f32[3,4096]{1,0:T(4,128)S(1)} %copy-done, s32[1,4096]{1,0:T(1,128)S(1)} %bitcast.3), custom_call_target="tpu_custom_call" | custom-call | tf_op jit(solution)/shard_map/sphere_velocities/pallas_call | solution.py:346
  (3 shorter events, 0.0 us)
Async XLA Ops:
  8.3 1.3 %copy-start.2 = (f32[4,128]{1,0:T(4,128)S(1)}, f32[4,128]{1,0:T(4,128)}, u32[]{:S(2)}) copy-start(f32[4,128]{1,0:T(4,128)} %inverse_ref.1) | copy-start | bytes 6148
  8.3 1.3 %collective-permute-start = (f32[48,128]{1,0:T(8,128)S(1)}, f32[48,128]{1,0:T(8,128)S(1)}, u32[]{:S(2)}, u32[]{:S(2)}) collective-permute-start(f32[48,128]{1,0:T(8,128)S(1)} %get-tuple-element.5), channel_id=1, source_target_pairs={{0,1},{1,0},{2,3},{3,2},{4,5},{5,4},{6,7},{7,6},{8,9},{9,8},{10,11... | collective-permute-start | bytes 73736 | tf_op jit(solution)/shard_map/ppermute | solution.py:270
  9.6 6.2 %collective-permute-start.3 = (f32[51,128]{1,0:T(8,128)S(1)}, f32[51,128]{1,0:T(8,128)S(1)}, u32[]{:S(2)}, u32[]{:S(2)}) collective-permute-start(f32[51,128]{1,0:T(8,128)S(1)} %core_sum.1.refs_0_), channel_id=1, source_target_pairs={{0,24},{2,26},{4,28},{6,30},{8,16},{10,18},{12,20},{14,22},{16,8},... | collective-permute-start | bytes 78344 | tf_op jit(solution)/shard_map/ppermute | solution.py:270
  13.8 3.9 %collective-permute-start.2 = (f32[51,128]{1,0:T(8,128)S(1)}, f32[51,128]{1,0:T(8,128)S(1)}, u32[]{:S(2)}, u32[]{:S(2)}) collective-permute-start(f32[51,128]{1,0:T(8,128)S(1)} %core_sum.1.refs_0_), channel_id=1, source_target_pairs={{0,8},{2,10},{4,12},{6,14},{8,0},{10,2},{12,4},{14,6},{16,24},{18,... | collective-permute-start | bytes 78344 | tf_op jit(solution)/shard_map/ppermute | solution.py:270
  14.7 4.8 %collective-permute-start.1 = (f32[51,128]{1,0:T(8,128)S(1)}, f32[51,128]{1,0:T(8,128)S(1)}, u32[]{:S(2)}, u32[]{:S(2)}) collective-permute-start(f32[51,128]{1,0:T(8,128)S(1)} %core_sum.1.refs_0_), channel_id=1, source_target_pairs={{0,16},{2,18},{4,20},{6,22},{8,24},{10,26},{12,28},{14,30},{16,0},... | collective-permute-start | bytes 78344 | tf_op jit(solution)/shard_map/ppermute | solution.py:270
  19.5 11.4 %copy-start = (f32[3,4096]{1,0:T(4,128)S(1)}, f32[3,4096]{1,0:T(4,128)}, u32[]{:S(2)}) copy-start(f32[3,4096]{1,0:T(4,128)} %offset_ref.1) | copy-start | bytes 147460
  19.5 11.4 %copy-start.1 = (s32[4096]{0:T(1024)S(1)}, s32[4096]{0:T(1024)}, u32[]{:S(2)}) copy-start(s32[4096]{0:T(1024)} %param.13) | copy-start | bytes 49156
  19.5 6.2 %collective-permute-start.6 = (f32[60,128]{1,0:T(8,128)S(1)}, f32[60,128]{1,0:T(8,128)S(1)}, u32[]{:S(2)}, u32[]{:S(2)}) collective-permute-start(f32[60,128]{1,0:T(8,128)S(1)} %space_sum.1.refs_0_), channel_id=1, source_target_pairs={{0,6},{2,4},{4,2},{6,0},{8,14},{10,12},{12,10},{14,8},{16,22},{18,... | collective-permute-start | bytes 92168 | tf_op jit(solution)/shard_map/ppermute | solution.py:270
  21.6 6.4 %collective-permute-start.5 = (f32[60,128]{1,0:T(8,128)S(1)}, f32[60,128]{1,0:T(8,128)S(1)}, u32[]{:S(2)}, u32[]{:S(2)}) collective-permute-start(f32[60,128]{1,0:T(8,128)S(1)} %space_sum.1.refs_0_), channel_id=1, source_target_pairs={{0,2},{2,0},{4,6},{6,4},{8,10},{10,8},{12,14},{14,12},{16,18},{18,... | collective-permute-start | bytes 92168 | tf_op jit(solution)/shard_map/ppermute | solution.py:270
  25.7 3.9 %collective-permute-start.4 = (f32[60,128]{1,0:T(8,128)S(1)}, f32[60,128]{1,0:T(8,128)S(1)}, u32[]{:S(2)}, u32[]{:S(2)}) collective-permute-start(f32[60,128]{1,0:T(8,128)S(1)} %space_sum.1.refs_0_), channel_id=1, source_target_pairs={{0,4},{2,6},{4,0},{6,2},{8,12},{10,14},{12,8},{14,10},{16,20},{18,... | collective-permute-start | bytes 92168 | tf_op jit(solution)/shard_map/ppermute | solution.py:270
  29.6 1.3 %collective-permute-start.7 = (f32[48,128]{1,0:T(8,128)S(1)}, f32[48,128]{1,0:T(8,128)S(1)}, u32[]{:S(2)}, u32[]{:S(2)}) collective-permute-start(f32[48,128]{1,0:T(8,128)S(1)} %clump_update.1.mine_ref), channel_id=1, source_target_pairs={{0,1},{1,0},{2,3},{3,2},{4,5},{5,4},{6,7},{7,6},{8,9},{9,8},{10,11... | collective-permute-start | bytes 73736 | tf_op jit(solution)/shard_map/ppermute | solution.py:270

commit v7 on v1

--- a/solution.py
+++ b/solution.py
@@ -11,6 +11,8 @@
 TILE = 128
 SLOT = 256
 UNROLL = 8
+FIRST_MOVES = ((1, 0, 3, 2), (3, 2, 0, 1), (2, 3, 1, 0))
+OTHER_MOVES = ((2, 3, 0, 1), (3, 0, 1, 2), (1, 2, 3, 0))
 LANES = 16
 BLOCK = TILE // LANES
 
@@ -75,8 +77,8 @@
 
     acc_ref[...] = jnp.zeros_like(acc_ref)
 
-    lane = lax.broadcasted_iota(jnp.int32, (TILE, 3 * TILE), 0)
-    target = lax.broadcasted_iota(jnp.int32, (TILE, 3 * TILE), 1) // TILE
+    lane = lax.broadcasted_iota(jnp.int32, (TILE, 2 * TILE), 0)
+    target = lax.broadcasted_iota(jnp.int32, (TILE, 2 * TILE), 1) // TILE
     part = lane % LANES
     wanted = (part == target) | (part == target + 3) | (part == target + 6)
     for j in range(BLOCK):
@@ -97,10 +99,14 @@
             high, low = split_two(jnp.concatenate([first, second], axis=0))
             both = jnp.concatenate([high, low], axis=0)
             terms_ref[tile] = jnp.concatenate([both, both], axis=1)
-            lines += [*split_three(state[0:3]), jnp.zeros((LANES - 9, TILE), f32)]
-        turned = jnp.concatenate(lines, axis=0).T.astype(bf16)
+            lines += [*split_three(state[0:3]), state[0:3], jnp.zeros((LANES - 12, TILE), f32)]
+        turned = jnp.concatenate(lines, axis=0).T
+        parts = turned.astype(bf16)
         for j in range(BLOCK):
-            wide_ref[block * BLOCK + j] = jnp.dot(turned, choose_ref[j], preferred_element_type=f32)
+            tile = block * BLOCK + j
+            z = j * LANES + 11
+            wide_ref[tile, :, 0 : 2 * TILE] = jnp.dot(parts, choose_ref[j], preferred_element_type=f32)
+            wide_ref[tile, :, 2 * TILE :] = jnp.broadcast_to(turned[:, z : z + 1], (TILE, TILE))
 
     copies[1].wait()
     place_ref[...] = sphere_ref[0:3, :] * (1.0 / support_radius) - 1.0
@@ -211,15 +217,23 @@
         out_ref[rows + k * more : rows + (k + 1) * more, :] = ref[rows:, :]
 
 
-def update_kernel(partners, *refs):
+def update_kernel(steps, *refs):
     *parts, out_ref, inverse_ref = refs
-    owners = len(partners)
+    owners = inverse_ref.shape[0]
     rows = 3 * owners
     held = owners // len(parts)
     me = lax.axis_index("space")
-    for k, partner in enumerate(partners):
+    holders = [0]
+    for stride, moves in steps:
+        radix = len(moves[0])
+        here = me // stride % radix
+        sources = [here]
+        for move in moves:
+            sources.append(sum(jnp.where(here == at, move.index(at), 0) for at in range(radix)))
+        holders = [holder + source * stride for source in sources for holder in holders]
+    for k, holder in enumerate(holders):
         first = rows + 3 * (k % held)
-        inverse_ref[me ^ partner] = parts[k // held][first : first + 3, :]
+        inverse_ref[holder] = parts[k // held][first : first + 3, :]
     out_ref[...] = sum_rows(parts, rows) * jnp.concatenate([inverse_ref[k] for k in range(owners)], axis=0)
 
 
@@ -255,9 +269,25 @@
     clump_ref[...] = velocity_ref[lax.axis_index("space")]
 
 
-def swap(value, axis, bit):
-    size = lax.axis_size(axis)
-    return lax.ppermute(value, axis, [(k, k ^ bit) for k in range(size)])
+def swap_cores(value):
+    return lax.ppermute(value, "sub", [(0, 1), (1, 0)])
+
+
+def send(value, stride, move):
+    pairs = []
+    for chip in range(lax.axis_size("space")):
+        digit = chip // stride % len(move)
+        pairs.append((chip, chip + (move[digit] - digit) * stride))
+    return lax.ppermute(value, "space", pairs)
+
+
+def steps_of(owners):
+    steps, stride = [], owners
+    while stride > 1:
+        radix = math.gcd(stride, 4)
+        stride //= radix
+        steps.append((stride, ((1, 0),) if radix == 2 else OTHER_MOVES if steps else FIRST_MOVES))
+    return steps
 
 
 def per_device(
@@ -274,7 +304,7 @@
     hbm = pl.BlockSpec(memory_space=pltpu.HBM)
     params = pltpu.CompilerParams(vmem_limit_bytes=48 * 1024 * 1024)
 
-    keep, send = pl.pallas_call(
+    keep, give = pl.pallas_call(
         loads_kernel,
         out_shape=(pltpu.VMEM((rows, clumps), f32), pltpu.VMEM((rows, clumps), f32)),
         in_specs=[pl.BlockSpec(memory_space=pltpu.SMEM)] + [hbm] * 7,
@@ -289,7 +319,7 @@
             pltpu.VMEM((4, clumps), f32),
             pltpu.SemaphoreType.DMA((7,)),
             pltpu.VMEM((3, spheres), f32),
-            pltpu.VMEM((BLOCK, TILE, 3 * TILE), bf16),
+            pltpu.VMEM((BLOCK, TILE, 2 * TILE), bf16),
             pltpu.VMEM((fluid // TILE, TILE, 3 * TILE), f32),
             pltpu.VMEM((fluid // TILE, 32, 2 * TILE), bf16),
             pltpu.VMEM((UNROLL, 2 * TILE, TILE), bf16),
@@ -315,21 +345,15 @@
             name=name,
         )(*operands)
 
-    mine = small(first_kernel, rows + 3, "core_sum", keep, swap(send, "sub", 1), clump_inverse)
-    bits = []
-    left = owners
-    while left > 1:
-        step = [left // 2, left // 4] if left > 2 else [1]
-        left //= 2 ** len(step)
-        bits += step
-        others = step if len(step) == 1 else [*step, sum(step)]
-        parts = [mine] + [swap(mine, "space", bit) for bit in others]
-        if left > 1:
+    mine = small(first_kernel, rows + 3, "core_sum", keep, swap_cores(give), clump_inverse)
+    steps = steps_of(owners)
+    for stride, moves in steps:
+        parts = [mine] + [send(mine, stride, move) for move in moves]
+        if stride > 1:
             height = rows + len(parts) * (mine.shape[0] - rows)
             mine = small(functools.partial(join_kernel, rows), height, "space_sum", *parts)
-    partners = [sum(bit for n, bit in enumerate(bits) if k >> n & 1) for k in range(owners)]
     velocities = small(
-        functools.partial(update_kernel, partners), rows, "clump_update", *parts,
+        functools.partial(update_kernel, steps), rows, "clump_update", *parts,
         scratch=[pltpu.VMEM((owners, 3, clumps), f32)],
     )
 
@@ -344,7 +368,7 @@
         scratch_shapes=[pltpu.VMEM((owners, 6, clumps), f32)],
         compiler_params=params,
         name="sphere_velocities",
-    )(velocities, swap(velocities, "sub", 1), sphere_offset, ids)
+    )(velocities, swap_cores(velocities), sphere_offset, ids)
 
 
 def solution(mesh):

time: 29.1 us -> 30.1 us (1.034)
  Pallas kernels: 6.62 us -> 7.53 us
    pallas_call x1, Pallas kernels: 5.66 us -> 6.55 us  [per_device(): pl.pallas_call(loads_kernel, out_shape=(pltpu.VMEM((rows, clumps), f32),...]
  transfers between devices with their start and end apart: 8 -> 8, of which waited for: 8 -> 6; matrix products, arithmetic and copies ran while one was open for 0% -> 0% of each run, Pallas kernels for 0% -> 0%
where the time goes in v7:
time: 30.1 us; the launch traced here: 29.8 us
  starting transfers between devices  10.5 us (35%)
  waiting for transfers between devices  10.4 us (35%)
  Pallas kernels  7.53 us (25%)
  between operations  1.36 us (5%)
    ppermute x6, starting transfers between devices, send(): return lax.ppermute(value, 'space', pairs)  10.4 us
    ppermute x6, waiting for transfers between devices, send(): return lax.ppermute(value, 'space', pairs)  8.05 us
    pallas_call x1, Pallas kernels, per_device(): pl.pallas_call(loads_kernel, out_shape=(pltpu.VMEM((rows, clumps), f32),...  6.55 us
    ppermute x2, waiting for transfers between devices, swap_cores(): return lax.ppermute(value, 'sub', [(0, 1), (1, 0)])  2.36 us
    pallas_call x1, Pallas kernels, per_device(): pl.pallas_call(velocity_kernel, out_shape=(jax.ShapeDtypeStruct((6, clump...  0.91 us
  transfers between devices with their start and end apart: 8, of which 6 were waited for; matrix products, arithmetic and copies ran while one was open for 0% of the time, Pallas kernels for 0%

profile of v7, /device:TPU:0, one launch (start us, length us, event | category | flops | bytes accessed | tf_op | source)
XLA Modules:
  0.0 29.8 jit_solution(6952209398607700182)
XLA Ops:
  1.3 6.5 %clump_loads.1 = (f32[48,128]{1,0:T(8,128)S(1)}, f32[48,128]{1,0:T(8,128)S(1)}) custom-call(s32[1]{0:T(128)S(6)} %copy.10.count_ref, s32[2,128]{1,0:T(2,128)} %bitcast.4, f32[8,4096]{1,0:T(8,128)} %fluid_hbm.1, f32[7,4096]{1,0:T(8,128)} %sphere_hbm.1, f32[3,4096]{1,0:T(4,128)} %offset_ref.1, s32[1,4096]{1,0:T(1,128)} %bitcast.2, f32[6,128]{1,0:T(8,128)} %state_hbm.1, ...), custom_call_target="tpu_custom_call" | custom-call | tf_op jit(solution)/shard_map/clump_loads/pallas_call | solution.py:307
  7.8 0.0 copy-start.2
  7.8 0.1 collective-permute-start
  7.9 1.2 %collective-permute-done.arrived_ref = f32[48,128]{1,0:T(8,128)S(1)} collective-permute-done((f32[48,128]{1,0:T(8,128)S(1)}, f32[48,128]{1,0:T(8,128)S(1)}, u32[]{:S(2)}, u32[]{:S(2)}) %collective-permute-start) | collective-permute-done | bytes 24608 | tf_op jit(solution)/shard_map/ppermute | solution.py:273
  9.1 0.0 copy-done.2
  9.1 6.8 %collective-permute-start.3 = (f32[51,128]{1,0:T(8,128)S(1)}, f32[51,128]{1,0:T(8,128)S(1)}, u32[]{:S(2)}, u32[]{:S(2)}) collective-permute-start(f32[51,128]{1,0:T(8,128)S(1)} %core_sum.1.refs_0_), channel_id=1, source_target_pairs={{0,16},{2,18},{4,20},{6,22},{8,24},{10,26},{12,28},{14,30},{16,8},... | collective-permute-start | bytes 78344 | tf_op jit(solution)/shard_map/ppermute | solution.py:281
  15.9 0.0 collective-permute-start.2
  15.9 0.6 %collective-permute-start.1 = (f32[51,128]{1,0:T(8,128)S(1)}, f32[51,128]{1,0:T(8,128)S(1)}, u32[]{:S(2)}, u32[]{:S(2)}) collective-permute-start(f32[51,128]{1,0:T(8,128)S(1)} %core_sum.1.refs_0_), channel_id=1, source_target_pairs={{0,8},{2,10},{4,12},{6,14},{8,0},{10,2},{12,4},{14,6},{16,24},{18,... | collective-permute-start | bytes 78344 | tf_op jit(solution)/shard_map/ppermute | solution.py:281
  16.5 0.9 %collective-permute-done.3.refs_3_ = f32[51,128]{1,0:T(8,128)S(1)} collective-permute-done((f32[51,128]{1,0:T(8,128)S(1)}, f32[51,128]{1,0:T(8,128)S(1)}, u32[]{:S(2)}, u32[]{:S(2)}) %collective-permute-start.3) | collective-permute-done | bytes 26144 | tf_op jit(solution)/shard_map/ppermute | solution.py:281
  17.5 3.2 %collective-permute-done.2.refs_2_ = f32[51,128]{1,0:T(8,128)S(1)} collective-permute-done((f32[51,128]{1,0:T(8,128)S(1)}, f32[51,128]{1,0:T(8,128)S(1)}, u32[]{:S(2)}, u32[]{:S(2)}) %collective-permute-start.2) | collective-permute-done | bytes 26144 | tf_op jit(solution)/shard_map/ppermute | solution.py:281
  20.7 0.0 collective-permute-done.1.refs_1_
  20.7 0.0 copy-start
  20.7 0.0 copy-start.1
  20.7 0.1 collective-permute-start.6
  20.8 2.9 %collective-permute-start.5 = (f32[60,128]{1,0:T(8,128)S(1)}, f32[60,128]{1,0:T(8,128)S(1)}, u32[]{:S(2)}, u32[]{:S(2)}) collective-permute-start(f32[60,128]{1,0:T(8,128)S(1)} %space_sum.1.refs_0_), channel_id=1, source_target_pairs={{0,6},{2,0},{4,2},{6,4},{8,14},{10,8},{12,10},{14,12},{16,22},{18,... | collective-permute-start | bytes 92168 | tf_op jit(solution)/shard_map/ppermute | solution.py:281
  23.7 0.0 collective-permute-start.4
  23.7 1.9 %collective-permute-done.6.refs_3_ = f32[60,128]{1,0:T(8,128)S(1)} collective-permute-done((f32[60,128]{1,0:T(8,128)S(1)}, f32[60,128]{1,0:T(8,128)S(1)}, u32[]{:S(2)}, u32[]{:S(2)}) %collective-permute-start.6) | collective-permute-done | bytes 30752 | tf_op jit(solution)/shard_map/ppermute | solution.py:281
  25.6 0.0 collective-permute-done.5.refs_2_
  25.6 2.0 %collective-permute-done.4.refs_1_ = f32[60,128]{1,0:T(8,128)S(1)} collective-permute-done((f32[60,128]{1,0:T(8,128)S(1)}, f32[60,128]{1,0:T(8,128)S(1)}, u32[]{:S(2)}, u32[]{:S(2)}) %collective-permute-start.4) | collective-permute-done | bytes 30752 | tf_op jit(solution)/shard_map/ppermute | solution.py:281
  27.6 0.1 clump_update.1.mine_ref
  27.7 0.1 collective-permute-start.7
  27.7 1.2 %collective-permute-done.7.arrived_ref = f32[48,128]{1,0:T(8,128)S(1)} collective-permute-done((f32[48,128]{1,0:T(8,128)S(1)}, f32[48,128]{1,0:T(8,128)S(1)}, u32[]{:S(2)}, u32[]{:S(2)}) %collective-permute-start.7) | collective-permute-done | bytes 24608 | tf_op jit(solution)/shard_map/ppermute | solution.py:273
  28.9 0.0 copy-done
  28.9 0.0 copy-done.1
  28.9 0.9 %sphere_velocities.1 = (f32[6,128]{1,0:T(8,128)}, f32[3,4096]{1,0:T(4,128)}) custom-call(f32[48,128]{1,0:T(8,128)S(1)} %clump_update.1.mine_ref, f32[48,128]{1,0:T(8,128)S(1)} %collective-permute-done.7.arrived_ref, f32[3,4096]{1,0:T(4,128)S(1)} %copy-done, s32[1,4096]{1,0:T(1,128)S(1)} %bitcast.3), custom_call_target="tpu_custom_call" | custom-call | tf_op jit(solution)/shard_map/sphere_velocities/pallas_call | solution.py:360
  (2 shorter events, 0.0 us)
Async XLA Ops:
  7.8 1.3 %copy-start.2 = (f32[4,128]{1,0:T(4,128)S(1)}, f32[4,128]{1,0:T(4,128)}, u32[]{:S(2)}) copy-start(f32[4,128]{1,0:T(4,128)} %inverse_ref.1) | copy-start | bytes 6148
  7.8 1.3 %collective-permute-start = (f32[48,128]{1,0:T(8,128)S(1)}, f32[48,128]{1,0:T(8,128)S(1)}, u32[]{:S(2)}, u32[]{:S(2)}) collective-permute-start(f32[48,128]{1,0:T(8,128)S(1)} %get-tuple-element.5), channel_id=1, source_target_pairs={{0,1},{1,0},{2,3},{3,2},{4,5},{5,4},{6,7},{7,6},{8,9},{9,8},{10,11... | collective-permute-start | bytes 73736 | tf_op jit(solution)/shard_map/ppermute | solution.py:273
  9.1 8.3 %collective-permute-start.3 = (f32[51,128]{1,0:T(8,128)S(1)}, f32[51,128]{1,0:T(8,128)S(1)}, u32[]{:S(2)}, u32[]{:S(2)}) collective-permute-start(f32[51,128]{1,0:T(8,128)S(1)} %core_sum.1.refs_0_), channel_id=1, source_target_pairs={{0,16},{2,18},{4,20},{6,22},{8,24},{10,26},{12,28},{14,30},{16,8},... | collective-permute-start | bytes 78344 | tf_op jit(solution)/shard_map/ppermute | solution.py:281
  15.9 4.8 %collective-permute-start.2 = (f32[51,128]{1,0:T(8,128)S(1)}, f32[51,128]{1,0:T(8,128)S(1)}, u32[]{:S(2)}, u32[]{:S(2)}) collective-permute-start(f32[51,128]{1,0:T(8,128)S(1)} %core_sum.1.refs_0_), channel_id=1, source_target_pairs={{0,24},{2,26},{4,28},{6,30},{8,16},{10,18},{12,20},{14,22},{16,0},... | collective-permute-start | bytes 78344 | tf_op jit(solution)/shard_map/ppermute | solution.py:281
  15.9 4.8 %collective-permute-start.1 = (f32[51,128]{1,0:T(8,128)S(1)}, f32[51,128]{1,0:T(8,128)S(1)}, u32[]{:S(2)}, u32[]{:S(2)}) collective-permute-start(f32[51,128]{1,0:T(8,128)S(1)} %core_sum.1.refs_0_), channel_id=1, source_target_pairs={{0,8},{2,10},{4,12},{6,14},{8,0},{10,2},{12,4},{14,6},{16,24},{18,... | collective-permute-start | bytes 78344 | tf_op jit(solution)/shard_map/ppermute | solution.py:281
  20.7 8.2 %copy-start = (f32[3,4096]{1,0:T(4,128)S(1)}, f32[3,4096]{1,0:T(4,128)}, u32[]{:S(2)}) copy-start(f32[3,4096]{1,0:T(4,128)} %offset_ref.1) | copy-start | bytes 147460
  20.7 8.2 %copy-start.1 = (s32[4096]{0:T(1024)S(1)}, s32[4096]{0:T(1024)}, u32[]{:S(2)}) copy-start(s32[4096]{0:T(1024)} %param.13) | copy-start | bytes 49156
  20.7 4.9 %collective-permute-start.6 = (f32[60,128]{1,0:T(8,128)S(1)}, f32[60,128]{1,0:T(8,128)S(1)}, u32[]{:S(2)}, u32[]{:S(2)}) collective-permute-start(f32[60,128]{1,0:T(8,128)S(1)} %space_sum.1.refs_0_), channel_id=1, source_target_pairs={{0,2},{2,4},{4,6},{6,0},{8,10},{10,12},{12,14},{14,8},{16,18},{18,... | collective-permute-start | bytes 92168 | tf_op jit(solution)/shard_map/ppermute | solution.py:281
  20.8 4.8 %collective-permute-start.5 = (f32[60,128]{1,0:T(8,128)S(1)}, f32[60,128]{1,0:T(8,128)S(1)}, u32[]{:S(2)}, u32[]{:S(2)}) collective-permute-start(f32[60,128]{1,0:T(8,128)S(1)} %space_sum.1.refs_0_), channel_id=1, source_target_pairs={{0,6},{2,0},{4,2},{6,4},{8,14},{10,8},{12,10},{14,12},{16,22},{18,... | collective-permute-start | bytes 92168 | tf_op jit(solution)/shard_map/ppermute | solution.py:281
  23.7 3.9 %collective-permute-start.4 = (f32[60,128]{1,0:T(8,128)S(1)}, f32[60,128]{1,0:T(8,128)S(1)}, u32[]{:S(2)}, u32[]{:S(2)}) collective-permute-start(f32[60,128]{1,0:T(8,128)S(1)} %space_sum.1.refs_0_), channel_id=1, source_target_pairs={{0,4},{2,6},{4,0},{6,2},{8,12},{10,14},{12,8},{14,10},{16,20},{18,... | collective-permute-start | bytes 92168 | tf_op jit(solution)/shard_map/ppermute | solution.py:281
  27.7 1.3 %collective-permute-start.7 = (f32[48,128]{1,0:T(8,128)S(1)}, f32[48,128]{1,0:T(8,128)S(1)}, u32[]{:S(2)}, u32[]{:S(2)}) collective-permute-start(f32[48,128]{1,0:T(8,128)S(1)} %clump_update.1.mine_ref), channel_id=1, source_target_pairs={{0,1},{1,0},{2,3},{3,2},{4,5},{5,4},{6,7},{7,6},{8,9},{9,8},{10,11... | collective-permute-start | bytes 73736 | tf_op jit(solution)/shard_map/ppermute | solution.py:273
